TPU v7x, 128 devices: a whole 4x4x4 slice. The times are simulated.
128 devices in a mesh: seq: 16 (over z, y_hi, core), blk: 8 (over y_lo, x).
Axes of the slice: x: 4, y: 4 (y_hi: 2, y_lo: 2; y = y_hi * 2 + y_lo), z: 4, core: 2. Of those that a mesh axis runs over, the one named last changes fastest.
Arguments:
- tokens: bfloat16 [16384, 8192], P('seq', 'blk'), may hold values from -6 to 6
- right_factor: bfloat16 [64, 128, 128], P('blk', 'seq'), may hold values from -0.5 to 0.5
- left_factor: bfloat16 [128, 64, 64], P('blk', 'seq'), may hold values from -0.75 to 0.75
- target: bfloat16 [16384, 8192], P('seq', 'blk'), may hold values from -4 to 4
Outputs:
- student: bfloat16 [16384, 8192], P('seq', 'blk')
- right_grad: float32 [64, 128, 128], P('blk', 'seq')
- left_grad: float32 [128, 64, 64], P('blk', 'seq')
All inputs are finite; a program needn't handle non-finite values.
Results may differ from a plain program's by a relative error of at most 0.017.
Values may be sent and summed in bfloat16 or wider, within the bound.
No kernel may reach another device: no remote copies, remote signals or barrier semaphores. Data moves between devices by JAX's collectives and lax.ppermute only.
A program may use at most 64 MiB of HBM per device.

v0:
```python
import jax
import jax.numpy as jnp
from jax import lax
from jax.sharding import PartitionSpec as P


def gelu_tanh(values):
    return jax.nn.gelu(values, approximate=True)


def shards(tokens, right_factor, left_factor, target):
    rows = tokens.shape[0]
    count = rows * lax.axis_size("seq")
    scale = 1.0 / jnp.sqrt(jnp.float32(count))
    right_full, left_full = (
        lax.all_gather(right_factor, "seq", axis=1, tiled=True),
        lax.all_gather(left_factor, "seq", axis=1, tiled=True),
    )
    nblocks = left_full.shape[1]
    local_blocks = right_full.shape[0]
    width = right_full.shape[1]
    inputs = tokens.reshape(rows, local_blocks, width)
    mixed = jnp.einsum(
        "tki,kci->tkc", inputs, right_full, preferred_element_type=jnp.float32
    ).astype(jnp.bfloat16)
    turned = lax.all_to_all(mixed, "blk", split_axis=2, concat_axis=1, tiled=True)
    turned, pre = (
        turned,
        jnp.einsum("tkc,cmk->tcm", turned, left_full, preferred_element_type=jnp.float32),
    )
    local_cols = pre.shape[1]
    act, back = jax.vjp(gelu_tanh, pre)
    student = act.reshape(rows, local_cols * nblocks).astype(jnp.bfloat16)
    residual = (act - target.reshape(rows, local_cols, nblocks).astype(jnp.float32)) * scale
    pre_grad = back(residual)[0].astype(jnp.bfloat16)
    turned_grad = jnp.einsum(
        "tcm,cmk->tkc", pre_grad, left_full, preferred_element_type=jnp.float32
    ).astype(jnp.bfloat16)
    mixed_grad = lax.all_to_all(turned_grad, "blk", split_axis=1, concat_axis=2, tiled=True)
    left_term = jnp.einsum("tcm,tkc->cmk", pre_grad, turned, preferred_element_type=jnp.float32)
    right_term = jnp.einsum("tkc,tki->kci", mixed_grad, inputs, preferred_element_type=jnp.float32)
    right_total, left_total = (
        lax.psum(right_term.astype(jnp.bfloat16), "seq").astype(jnp.float32),
        lax.psum(left_term.astype(jnp.bfloat16), "seq").astype(jnp.float32),
    )
    place = lax.axis_index("seq")
    right_rows = right_factor.shape[1]
    left_rows = left_factor.shape[1]
    right_grad = lax.dynamic_slice_in_dim(right_total, place * right_rows, right_rows, 1)
    left_grad = lax.dynamic_slice_in_dim(left_total, place * left_rows, left_rows, 1)
    return (student, right_grad, left_grad)


def solution(mesh):
    return jax.shard_map(
        shards,
        mesh=mesh,
        in_specs=(P("seq", "blk"), P("blk", "seq", None), P("blk", "seq", None), P("seq", "blk")),
        out_specs=(P("seq", "blk"), P("blk", "seq", None), P("blk", "seq", None)),
        check_vma=False,
    )
```

profile of v0, /device:TPU:0, one launch (start us, length us, event | category | flops | bytes accessed | tf_op | source)
XLA Modules:
  0.0 279.8 jit_solution(13000971417474091226)
XLA Ops:
  7.2 0.0 copy-start
  7.2 27.1 %all_gather.6 = bf16[8,128,128]{2,1,0:T(8,128)(2,1)S(1)} all-gather(bf16[8,8,128]{2,1,0:T(8,128)(2,1)} %param.5), channel_id=1, replica_groups=mesh['seq'=16,'blk'=8] {'seq'}, dimensions={1}, use_global_device_ids=true | all-gather | bytes 278528 | tf_op jit(solution)/shard_map/all_gather | solution.py:16
  34.3 0.0 copy-done
  34.3 0.7 convert_bitcast_fusion.1
  35.0 2.5 copy.14
  37.5 0.0 copy-start.2
  37.5 4.5 %all-to-all-start = ((bf16[1024,8,128]{0,1,2:T(8,128)(2,1)}), bf16[1024,8,128]{0,1,2:T(8,128)(2,1)}, u32[]{:S(2)}, u32[]{:S(2)}) async-start(bf16[1024,8,128]{0,1,2:T(8,128)(2,1)} %copy.14), calls=%async_computation | async-start | bytes 4194304 | tf_op jit(solution)/shard_map/all_to_all | solution.py:26
  42.0 0.0 copy-done.2
  42.0 4.1 %copy.18 = f32[1024,1024]{0,1:T(8,128)} copy(bf16[1024,1024]{1,0:T(8,128)(2,1)} %param.7) | data formatting | bytes 6291456 | tf_op jit(solution)/shard_map/convert_element_type | solution.py:34
  46.2 31.9 %all_gather.7 = bf16[16,64,64]{2,0,1:T(8,128)(2,1)S(1)} all-gather(bf16[16,4,64]{2,0,1:T(8,128)(2,1)S(1)} %copy.16), channel_id=1, replica_groups=mesh['seq'=16,'blk'=8] {'seq'}, dimensions={1}, use_global_device_ids=true | all-gather | bytes 139264 | tf_op jit(solution)/shard_map/all_gather | solution.py:17
  78.1 0.0 all-to-all-done
  78.1 7.1 %fusion.6 = (bf16[1024,16,64]{0,2,1:T(8,128)(2,1)S(1)}, bf16[1024,16,64]{0,2,1:T(8,128)(2,1)}) fusion(f32[1024,16,64]{0,2,1:T(8,128)} %bitcast.61, bf16[1024,8,8,16]{0,1,3,2:T(8,128)(2,1)} %bitcast.1, bf16[16,64,64]{2,0,1:T(8,128)(2,1)S(1)} %all_gather.7), kind=kOutput, calls=%fused_computation.8 | convolution fusion | flops 159383552 | bytes 10616832 | tf_op jit(solution)/shard_map/tkc,cmk->tcm/dot_general | solution.py:29
  85.1 0.0 copy-start.1
  85.1 0.8 convert_bitcast_fusion
  85.9 0.6 copy-done.1
  86.4 2.5 copy.20
  88.9 11.3 %all-to-all-start.1 = ((bf16[1024,64,16]{0,2,1:T(8,128)(2,1)}), bf16[1024,64,16]{0,2,1:T(8,128)(2,1)}, u32[]{:S(2)}, u32[]{:S(2)}) async-start(bf16[1024,64,16]{0,2,1:T(8,128)(2,1)} %copy.20), calls=%async_computation.1 | async-start | bytes 4194304 | tf_op jit(solution)/shard_map/all_to_all | solution.py:39
  100.2 0.0 all-reduce.3.cloned.1.call-start
  100.3 3.7 %fusion.24 = bf16[16,64,64]{2,1,0:T(8,128)(2,1)} fusion(bf16[1024,16,64]{0,2,1:T(8,128)(2,1)} %copy-done.1, bf16[1024,8,8,16]{0,1,3,2:T(8,128)(2,1)} %bitcast.1), kind=kOutput, calls=%fused_computation.28 | convolution fusion | flops 134283264 | bytes 4325376 | tf_op jit(solution)/shard_map/tcm,tkc->cmk/dot_general | solution.py:40
  103.9 23.8 %all-to-all-done.1 = bf16[1024,64,16]{0,2,1:T(8,128)(2,1)} async-done(((bf16[1024,64,16]{0,2,1:T(8,128)(2,1)}), bf16[1024,64,16]{0,2,1:T(8,128)(2,1)}, u32[]{:S(2)}, u32[]{:S(2)}) %all-to-all-start.1) | async-done | bytes 2097184 | tf_op jit(solution)/shard_map/all_to_all | solution.py:39
  127.8 1.8 copy.21
  129.6 1.5 fusion.27
  131.1 0.0 all-reduce.3.cloned.1.call-update
  131.1 3.9 %copy.23 = bf16[1024,1024]{1,0:T(8,128)(2,1)} copy(bf16[1024,1024]{0,1:T(8,128)(2,1)} %bitcast.62) | data formatting | bytes 4194304
  135.1 135.2 %all-reduce.3.cloned.1.call-done = (bf16[8,128,128]{2,1,0:T(8,128)(2,1)}, bf16[16,64,64]{2,1,0:T(8,128)(2,1)}) async-done(((bf16[8,128,128]{2,1,0:T(8,128)(2,1)}, bf16[16,64,64]{2,1,0:T(8,128)(2,1)}), (bf16[8,128,128]{2,1,0:T(8,128)(2,1)}, bf16[16,64,64]{2,1,0:T(8,128)(2,1)})) %all-reduce.3.cloned.1.call-update) | async-done | bytes 393232 | tf_op jit(solution)/shard_map/psum | solution.py:43
  270.2 1.4 dynamic-slice_convert_fusion
  271.6 1.3 dynamic-slice_convert_fusion.1
  (1 shorter events, 0.0 us)
Async XLA Ops:
  7.2 27.1 %copy-start = (bf16[1024,1024]{1,0:T(8,128)(2,1)S(1)}, bf16[1024,1024]{1,0:T(8,128)(2,1)}, u32[]{:S(2)}) copy-start(bf16[1024,1024]{1,0:T(8,128)(2,1)} %param.4) | copy-start | bytes 6291460
  37.5 4.5 %copy-start.2 = (bf16[16,4,64]{2,1,0:T(4,128)(2,1)S(1)}, bf16[16,4,64]{2,1,0:T(4,128)(2,1)}, u32[]{:S(2)}) copy-start(bf16[16,4,64]{2,1,0:T(4,128)(2,1)} %param.6) | copy-start | bytes 24580
  37.5 40.6 %all-to-all-start = ((bf16[1024,8,128]{0,1,2:T(8,128)(2,1)}), bf16[1024,8,128]{0,1,2:T(8,128)(2,1)}, u32[]{:S(2)}, u32[]{:S(2)}) async-start(bf16[1024,8,128]{0,1,2:T(8,128)(2,1)} %copy.14), calls=%async_computation | async-start | bytes 4194304 | tf_op jit(solution)/shard_map/all_to_all | solution.py:26
  85.1 1.3 copy-start.1
  88.9 38.9 %all-to-all-start.1 = ((bf16[1024,64,16]{0,2,1:T(8,128)(2,1)}), bf16[1024,64,16]{0,2,1:T(8,128)(2,1)}, u32[]{:S(2)}, u32[]{:S(2)}) async-start(bf16[1024,64,16]{0,2,1:T(8,128)(2,1)} %copy.20), calls=%async_computation.1 | async-start | bytes 4194304 | tf_op jit(solution)/shard_map/all_to_all | solution.py:39
  100.2 170.0 %all-reduce.3.cloned.1.call-start = ((), (), s32[]{:S(2)}) async-start(), calls=%async_computation.2 | async-start | bytes 1048576 | tf_op jit(solution)/shard_map/psum | solution.py:43
Sparse Core Ops, SparseCore 0:
  131.2 138.9 all-reduce.2
where the time goes:
time: 281 us; the launch traced here: 280 us
  waiting for transfers between devices  159 us (57%)
  blocking collectives  59 us (21%)
  starting transfers between devices  15.9 us (6%)
  local copies, waits for them, and re-layouts  15.4 us (5%)
  between operations  14.1 us (5%)
  matrix products  13.8 us (5%)
    psum x1, waiting for transfers between devices, shards(): lax.psum(right_term.astype(jnp.bfloat16), 'seq').astype(jnp.float32)  135 us
    all_gather x1, blocking collectives, shards(): lax.all_gather(left_factor, 'seq', axis=1, tiled=True)  31.9 us
    all_gather x1, blocking collectives, shards(): lax.all_gather(right_factor, 'seq', axis=1, tiled=True)  27.1 us
    all_to_all x1, waiting for transfers between devices, shards(): lax.all_to_all(turned_grad, 'blk', split_axis=1, concat_axis=2, tiled=True)  23.8 us
    all_to_all x1, starting transfers between devices, shards(): lax.all_to_all(turned_grad, 'blk', split_axis=1, concat_axis=2, tiled=True)  11.3 us
    dot_general x1, matrix products, shards(): jnp.einsum('tkc,cmk->tcm', turned, left_full, preferred_element_type=jnp....  7.07 us
  transfers between devices with their start and end apart: 3, of which 2 were waited for; matrix products, arithmetic and copies ran while one was open for 4% of the time, Pallas kernels for 0%

commit v1 on v0

v1 whole, which is shorter than its diff:
```python
import functools
import math

import jax
import jax.numpy as jnp
from jax import lax
from jax.experimental import pallas as pl
from jax.experimental.pallas import tpu as pltpu
from jax.sharding import PartitionSpec as P

BF = jnp.bfloat16
F32 = jnp.float32
MIB = 1 << 20
ROOT = math.sqrt(2.0 / math.pi)
CUBE = 0.044715


def iota(shape, dim):
    return lax.broadcasted_iota(jnp.int32, shape, dim)


def cost(flops, size):
    return pl.CostEstimate(flops=int(flops), bytes_accessed=int(size), transcendentals=0)


def dot(a, b, dims=((1,), (0,))):
    return lax.dot_general(a, b, (dims, ((), ())), preferred_element_type=F32)


def params(limit=24):
    return pltpu.CompilerParams(vmem_limit_bytes=limit * MIB)


def mix_kernel(x_ref, g_ref, out_ref, big_ref):
    width = 1024

    @pl.when(pl.program_id(0) == 0)
    def _():
        flat = jnp.concatenate([g_ref[s, 0:64, :].astype(F32) for s in range(16)], axis=0)
        turned = flat.T
        lane_k = (iota((128, width), 1) >> 3) & 7
        for k in range(8):
            big_ref[k * 128 : (k + 1) * 128, :] = jnp.where(lane_k == k, turned, 0.0).astype(BF)

    mixed = dot(x_ref[...], big_ref[...]).astype(BF)
    for j in range(8):
        out_ref[j] = mixed[:, j * 128 : (j + 1) * 128]


def mix(x, gathered):
    rows = x.shape[0]
    step = 256
    return pl.pallas_call(
        mix_kernel,
        grid=(rows // step,),
        in_specs=[
            pl.BlockSpec((step, 1024), lambda t: (t, 0)),
            pl.BlockSpec((16, 96, 128), lambda t: (0, 0, 0)),
        ],
        out_specs=pl.BlockSpec((8, step, 128), lambda t: (0, t, 0)),
        out_shape=jax.ShapeDtypeStruct((8, rows, 128), BF),
        scratch_shapes=[pltpu.VMEM((1024, 1024), BF)],
        compiler_params=params(),
        cost_estimate=cost(2 * rows * 1024 * 1024, 4 * rows * 1024),
        name="mix",
    )(x, gathered)


def permutation():
    r, q = iota((512, 512), 0), iota((512, 512), 1)
    here = ((r >> 6) == ((q >> 2) & 7)) & (((r >> 2) & 15) == (q >> 5)) & ((r & 3) == (q & 3))
    return here.astype(F32).astype(BF)


def spread(h):
    r, f = iota((128, 1024), 0), iota((128, 1024), 1)
    k = ((f >> 7) << 3) + ((f >> 3) & 7)
    return (r == k + h * 64).astype(F32).astype(BF)


def column_block(f):
    return (((f >> 6) & 1) << 3) + (f & 7)


def expand_kernel(g_ref, wide_ref, back_ref):
    packed = jnp.concatenate([g_ref[s, 64:96, :] for s in range(16)], axis=0)
    ordered = dot(permutation(), packed)
    turned = ordered.T.astype(BF)
    ordered = ordered.astype(BF)
    for h in range(2):
        once = spread(h)
        row_c = (iota((512, 1024), 0) >> 6) + h * 8
        match = row_c == column_block(iota((512, 1024), 1))
        back_ref[h * 512 : (h + 1) * 512, :] = jnp.where(match, dot(ordered, once), 0.0).astype(BF)
        col_c = (iota((1024, 512), 1) >> 6) + h * 8
        match = col_c == column_block(iota((1024, 512), 0))
        full = dot(once, turned, ((0,), (0,)))
        wide_ref[:, h * 512 : (h + 1) * 512] = jnp.where(match, full, 0.0).astype(BF)


def expand(gathered):
    shape = jax.ShapeDtypeStruct((1024, 1024), BF)
    return pl.pallas_call(
        expand_kernel,
        out_shape=(shape, shape),
        compiler_params=params(40),
        cost_estimate=cost(2 * 1024 * 1024 * 1024, 4 * MIB),
        name="expand",
    )(gathered)


def turn_kernel(x_ref, out_ref):
    out_ref[...] = x_ref[...].T


def turn(x):
    rows, width = x.shape
    step = 256
    return pl.pallas_call(
        turn_kernel,
        grid=(width // step,),
        in_specs=[pl.BlockSpec((rows, step), lambda f: (0, f))],
        out_specs=pl.BlockSpec((step, rows), lambda f: (f, 0)),
        out_shape=jax.ShapeDtypeStruct((width, rows), BF),
        compiler_params=params(),
        cost_estimate=cost(2 * rows * 1024 * 1024, 4 * rows * 1024),
        name="turn",
    )(x)


def middle_kernel(scale, in_ref, wide_ref, back_ref, target_ref, student_ref, grad_ref, out_ref):
    turned = jnp.concatenate([in_ref[j] for j in range(8)], axis=1)
    v = dot(turned, wide_ref[...])
    square = v * v
    p = 0.5 + 0.5 * jnp.tanh(v * (ROOT + (ROOT * CUBE) * square))
    act = v * p
    slope = p + (act - act * p) * (2.0 * ROOT + (6.0 * ROOT * CUBE) * square)
    student_ref[...] = act.astype(BF)
    grad = ((act - target_ref[...].astype(F32)) * (slope * scale)).astype(BF)
    grad_ref[...] = grad
    out = dot(grad, back_ref[...]).astype(BF)
    for j in range(8):
        out_ref[j] = out[:, j * 128 : (j + 1) * 128]


def middle(received, wide, back, target, scale):
    rows = target.shape[0]
    step = 256
    block = pl.BlockSpec((8, step, 128), lambda t: (0, t, 0))
    line = pl.BlockSpec((step, 1024), lambda t: (t, 0))
    whole = pl.BlockSpec((1024, 1024), lambda t: (0, 0))
    flat = jax.ShapeDtypeStruct((rows, 1024), BF)
    return pl.pallas_call(
        functools.partial(middle_kernel, scale),
        grid=(rows // step,),
        in_specs=[block, whole, whole, line],
        out_specs=(line, line, block),
        out_shape=(flat, flat, jax.ShapeDtypeStruct((8, rows, 128), BF)),
        compiler_params=params(40),
        cost_estimate=cost(4 * rows * 1024 * 1024, 10 * rows * 1024),
        name="middle",
    )(received, wide, back, target)


def left_kernel(grad_ref, in_ref, out_ref, total_ref):
    step = pl.program_id(0)
    h = step // 2
    turned = jnp.concatenate([in_ref[j] for j in range(8)], axis=1)
    full = dot(grad_ref[...], turned, ((0,), (0,)))
    row_c = (iota((256, 1024), 0) >> 6) + step * 4
    full = jnp.where(row_c == column_block(iota((256, 1024), 1)), full, 0.0).astype(BF)
    kept = dot(full, spread(h), ((1,), (1,)))
    place = pl.ds(pl.multiple_of((step % 2) * 256, 256), 256)

    @pl.when(step < 2)
    def _():
        total_ref[place, :] = kept

    @pl.when(step >= 2)
    def _():
        total_ref[place, :] += kept

    @pl.when(step == 3)
    def _():
        ordered = dot(permutation(), total_ref[...].astype(BF), ((0,), (0,))).astype(BF)
        for s in range(16):
            out_ref[s] = ordered[s * 32 : (s + 1) * 32, :]


def left_grads(grad, received):
    rows = grad.shape[0]
    return pl.pallas_call(
        left_kernel,
        grid=(4,),
        in_specs=[
            pl.BlockSpec((rows, 256), lambda n: (0, n)),
            pl.BlockSpec((8, rows, 128), lambda n: (0, 0, 0)),
        ],
        out_specs=pl.BlockSpec((16, 32, 128), lambda n: (0, 0, 0)),
        out_shape=jax.ShapeDtypeStruct((16, 32, 128), BF),
        scratch_shapes=[pltpu.VMEM((512, 128), F32)],
        compiler_params=params(40),
        cost_estimate=cost(4 * rows * 1024 * 1024, 4 * rows * 1024),
        name="left_grads",
    )(grad, received)


def right_kernel(in_ref, turned_ref, left_ref, out_ref):
    pair = jnp.concatenate([in_ref[0], in_ref[1]], axis=1)
    full = dot(turned_ref[...], pair)
    lane_k = (iota((128, 256), 1) >> 3) & 7
    kept = jnp.zeros((128, 256), F32)
    for k in range(8):
        kept = jnp.where(lane_k == k, full[k * 128 : (k + 1) * 128, :], kept)
    kept = kept.T.astype(BF)
    for s in range(4):
        out_ref[s, 0:64, :] = kept[s * 64 : (s + 1) * 64, :]
        out_ref[s, 64:96, :] = left_ref[s]


def right_grads(received, turned, left):
    rows = turned.shape[1]
    return pl.pallas_call(
        right_kernel,
        grid=(4,),
        in_specs=[
            pl.BlockSpec((2, rows, 128), lambda n: (n, 0, 0)),
            pl.BlockSpec((1024, rows), lambda n: (0, 0)),
            pl.BlockSpec((4, 32, 128), lambda n: (n, 0, 0)),
        ],
        out_specs=pl.BlockSpec((4, 96, 128), lambda n: (n, 0, 0)),
        out_shape=jax.ShapeDtypeStruct((16, 96, 128), BF),
        compiler_params=params(40),
        cost_estimate=cost(2 * rows * 1024 * 1024, 4 * rows * 1024),
        name="right_grads",
    )(received, turned, left)


def shards(tokens, right_factor, left_factor, target):
    rows = tokens.shape[0]
    scale = 1.0 / math.sqrt(rows * lax.axis_size("seq"))
    packed = jnp.concatenate(
        [
            right_factor.reshape(64, 128),
            jnp.concatenate([left_factor[:8], left_factor[8:]], axis=2).reshape(32, 128),
        ],
        axis=0,
    )
    gathered = lax.all_to_all(jnp.broadcast_to(packed, (16, 96, 128)), "seq", 0, 0, tiled=True)
    mixed = mix(tokens, gathered)
    received = lax.all_to_all(mixed, "blk", 0, 0, tiled=True)
    wide, back = expand(gathered)
    turned = turn(tokens)
    student, grad, out = middle(received, wide, back, target, scale)
    returned = lax.all_to_all(out, "blk", 0, 0, tiled=True)
    left = left_grads(grad, received)
    terms = right_grads(returned, turned, left)
    terms = lax.all_to_all(terms, "seq", 0, 0, tiled=True)
    total = jnp.sum(terms.astype(F32), axis=0)
    right_grad = total[:64].reshape(8, 8, 128)
    left_total = total[64:].reshape(8, 4, 2, 64)
    left_grad = jnp.transpose(left_total, (2, 0, 1, 3)).reshape(16, 4, 64)
    return (student, right_grad, left_grad)


def solution(mesh):
    return jax.shard_map(
        shards,
        mesh=mesh,
        in_specs=(P("seq", "blk"), P("blk", "seq", None), P("blk", "seq", None), P("seq", "blk")),
        out_specs=(P("seq", "blk"), P("blk", "seq", None), P("blk", "seq", None)),
        check_vma=False,
    )
```

time: 281 us -> 131 us (0.47)
  waiting for transfers between devices: 159 us -> 40.2 us
  Pallas kernels: 0 us -> 23 us
  blocking collectives: 59 us -> 37 us
  matrix products: 13.8 us -> 0 us
  between operations: 14.1 us -> 0.74 us
  starting transfers between devices: 15.9 us -> 8.75 us
  local copies, waits for them, and re-layouts: 15.4 us -> 19.7 us
    psum x1 -> x0, waiting for transfers between devices: 135 us -> none  [shards(): lax.psum(right_term.astype(jnp.bfloat16), 'seq').astype(jnp.float32)]
    all_gather x2 -> x0, blocking collectives: 59 us -> none  [the longest x1 31.9 us: shards(): lax.all_gather(left_factor, 'seq', axis=1, tiled=True)]
    all_to_all x0 -> x2, blocking collectives: none -> 37 us  [the longest x1 18.9 us: shards(): lax.all_to_all(jnp.broadcast_to(packed, (16, 96, 128)), 'seq', 0, 0, tile...]
    pallas_call x0 -> x6, Pallas kernels: none -> 23 us  [the longest x1 7.52 us: middle(): pl.pallas_call(functools.partial(middle_kernel, scale), grid=(rows // ste...]
    all_to_all x2, waiting for transfers between devices: 23.8 us -> 40.2 us  [the longest x1 22 us: shards(): received = lax.all_to_all(mixed, 'blk', 0, 0, tiled=True)]
    dot_general x5 -> x0, matrix products: 13.8 us -> none  [the longest x1 7.07 us: shards(): jnp.einsum('tkc,cmk->tcm', turned, left_full, preferred_element_type=jnp....]
    unnamed x8 -> x27, local copies, waits for them, and re-layouts: 4.52 us -> 18.2 us
    convert_element_type x3 -> x0, local copies, waits for them, and re-layouts: 9.08 us -> none  [the longest x1 4.14 us: shards(): target.reshape(rows, local_cols, nblocks).astype(jnp.float32)]
  transfers between devices with their start and end apart: 3 -> 2, of which waited for: 2 -> 2; matrix products, arithmetic and copies ran while one was open for 4% -> 0% of each run, Pallas kernels for 0% -> 6%
where the time goes in v1:
time: 131 us; the launch traced here: 130 us
  waiting for transfers between devices  40.2 us (31%)
  blocking collectives  37 us (28%)
  Pallas kernels  23 us (18%)
  local copies, waits for them, and re-layouts  19.7 us (15%)
  starting transfers between devices  8.75 us (7%)
    all_to_all x1, waiting for transfers between devices, shards(): received = lax.all_to_all(mixed, 'blk', 0, 0, tiled=True)  22 us
    all_to_all x1, blocking collectives, shards(): lax.all_to_all(jnp.broadcast_to(packed, (16, 96, 128)), 'seq', 0, 0, tile...  18.9 us
    all_to_all x1, waiting for transfers between devices, shards(): returned = lax.all_to_all(out, 'blk', 0, 0, tiled=True)  18.2 us
    unnamed x27, local copies, waits for them, and re-layouts  18.2 us
    all_to_all x1, blocking collectives, shards(): terms = lax.all_to_all(terms, 'seq', 0, 0, tiled=True)  18.1 us
    pallas_call x1, Pallas kernels, middle(): pl.pallas_call(functools.partial(middle_kernel, scale), grid=(rows // ste...  7.52 us
    pallas_call x1, Pallas kernels, left_grads(): pl.pallas_call(left_kernel, grid=(4,), in_specs=[pl.BlockSpec((rows, 256)...  4.76 us
    pallas_call x1, Pallas kernels, right_grads(): pl.pallas_call(right_kernel, grid=(4,), in_specs=[pl.BlockSpec((2, rows,...  4.49 us
  transfers between devices with their start and end apart: 2, of which 2 were waited for; matrix products, arithmetic and copies ran while one was open for 0% of the time, Pallas kernels for 6%

profile of v1, /device:TPU:0, one launch (start us, length us, event | category | flops | bytes accessed | tf_op | source)
XLA Modules:
  0.0 130.3 jit_solution(8977202113056069033)
XLA Ops:
  0.6 0.7 fusion
  1.4 0.1 pad_maximum_fusion.1
  1.4 0.7 pad_maximum_fusion
  2.2 0.1 broadcast_in_dim.3
  2.2 18.9 %all_to_all.20.g_ref = bf16[16,96,128]{2,1,0:T(8,128)(2,1)S(1)} all-to-all(bf16[16,96,128]{2,1,0:T(8,128)(2,1)S(1)} %broadcast_in_dim.3), channel_id=1, replica_groups=mesh['seq'=16,'blk'=8] {'seq'}, dimensions={0} | all-to-all | bytes 786432 | tf_op jit(solution)/shard_map/all_to_all | solution.py:249
  21.1 1.6 %copy-done.3 = bf16[1024,1024]{1,0:T(8,128)(2,1)S(1)} copy-done((bf16[1024,1024]{1,0:T(8,128)(2,1)S(1)}, bf16[1024,1024]{1,0:T(8,128)(2,1)}, u32[]{:S(2)}) %copy-start.3) | copy-done | bytes 2097176
  22.7 3.4 %mix.1 = bf16[8,1024,128]{2,1,0:T(8,128)(2,1)S(1)} custom-call(bf16[1024,1024]{1,0:T(8,128)(2,1)S(1)} %copy-done.3, bf16[16,96,128]{2,1,0:T(8,128)(2,1)S(1)} %all_to_all.20.g_ref), custom_call_target="tpu_custom_call" | custom-call | flops 2147483648 | bytes 4194304 | tf_op jit(solution)/shard_map/mix/pallas_call | solution.py:53
  26.1 1.3 %copy-done.1 = bf16[8,1024,128]{2,1,0:T(8,128)(2,1)} copy-done((bf16[8,1024,128]{2,1,0:T(8,128)(2,1)}, bf16[8,1024,128]{2,1,0:T(8,128)(2,1)S(1)}, u32[]{:S(2)}) %copy-start.1) | copy-done | bytes 2097176
  27.4 4.4 %all-to-all-start.1 = ((bf16[8,1024,128]{2,1,0:T(8,128)(2,1)}), bf16[8,1024,128]{2,1,0:T(8,128)(2,1)S(1)}, u32[]{:S(2)}, u32[]{:S(2)}) async-start(bf16[8,1024,128]{2,1,0:T(8,128)(2,1)} %copy-done.1), calls=%async_computation.1 | async-start | bytes 4194304 | tf_op jit(solution)/shard_map/all_to_all | solution.py:251
  31.8 1.8 %expand.1 = (bf16[1024,1024]{1,0:T(8,128)(2,1)S(1)}, bf16[1024,1024]{1,0:T(8,128)(2,1)S(1)}) custom-call(bf16[16,96,128]{2,1,0:T(8,128)(2,1)S(1)} %all_to_all.20.g_ref), custom_call_target="tpu_custom_call" | custom-call | flops 2147483648 | bytes 4194304 | tf_op jit(solution)/shard_map/expand/pallas_call | solution.py:103
  33.6 1.3 %copy-done.9 = bf16[1024,1024]{1,0:T(8,128)(2,1)} copy-done((bf16[1024,1024]{1,0:T(8,128)(2,1)}, bf16[1024,1024]{1,0:T(8,128)(2,1)S(1)}, u32[]{:S(2)}) %copy-start.9) | copy-done | bytes 2097176
  34.9 1.3 %copy-done.11 = bf16[1024,1024]{1,0:T(8,128)(2,1)} copy-done((bf16[1024,1024]{1,0:T(8,128)(2,1)}, bf16[1024,1024]{1,0:T(8,128)(2,1)S(1)}, u32[]{:S(2)}) %copy-start.11) | copy-done | bytes 2097176
  36.3 22.0 %all-to-all-done.1.in_ref = bf16[8,1024,128]{2,1,0:T(8,128)(2,1)S(1)} async-done(((bf16[8,1024,128]{2,1,0:T(8,128)(2,1)}), bf16[8,1024,128]{2,1,0:T(8,128)(2,1)S(1)}, u32[]{:S(2)}, u32[]{:S(2)}) %all-to-all-start.1) | async-done | bytes 2097184 | tf_op jit(solution)/shard_map/all_to_all | solution.py:251
  58.3 1.6 %copy-done.2 = bf16[1024,1024]{1,0:T(8,128)(2,1)S(1)} copy-done((bf16[1024,1024]{1,0:T(8,128)(2,1)S(1)}, bf16[1024,1024]{1,0:T(8,128)(2,1)}, u32[]{:S(2)}) %copy-start.2) | copy-done | bytes 2097176
  59.9 1.6 %copy-done.10 = bf16[1024,1024]{1,0:T(8,128)(2,1)S(1)} copy-done((bf16[1024,1024]{1,0:T(8,128)(2,1)S(1)}, bf16[1024,1024]{1,0:T(8,128)(2,1)}, u32[]{:S(2)}) %copy-start.10) | copy-done | bytes 2097176
  61.4 1.6 %copy-done.12 = bf16[1024,1024]{1,0:T(8,128)(2,1)S(1)} copy-done((bf16[1024,1024]{1,0:T(8,128)(2,1)S(1)}, bf16[1024,1024]{1,0:T(8,128)(2,1)}, u32[]{:S(2)}) %copy-start.12) | copy-done | bytes 2097176
  63.0 7.5 %middle.1 = (bf16[1024,1024]{1,0:T(8,128)(2,1)}, bf16[1024,1024]{1,0:T(8,128)(2,1)S(1)}, bf16[8,1024,128]{2,1,0:T(8,128)(2,1)S(1)}) custom-call(bf16[8,1024,128]{2,1,0:T(8,128)(2,1)S(1)} %all-to-all-done.1.in_ref, bf16[1024,1024]{1,0:T(8,128)(2,1)S(1)} %copy-done.10, bf16[1024,1024]{1,0:T(8,128)(2,1)S(1)} %copy-done.12, bf16[1024,1024]{1,0:T(8,128)(2,1)S(1)} %copy-done.2), custom_call_target="tpu_custom_call" | custom-call | flops 4294967296 | bytes 10485760 | tf_op jit(solution)/shard_map/middle/pallas_call | solution.py:153
  70.6 1.3 %copy-done = bf16[8,1024,128]{2,1,0:T(8,128)(2,1)} copy-done((bf16[8,1024,128]{2,1,0:T(8,128)(2,1)}, bf16[8,1024,128]{2,1,0:T(8,128)(2,1)S(1)}, u32[]{:S(2)}) %copy-start) | copy-done | bytes 2097176
  71.9 1.3 %copy-done.7 = bf16[1024,1024]{1,0:T(8,128)(2,1)} copy-done((bf16[1024,1024]{1,0:T(8,128)(2,1)}, bf16[1024,1024]{1,0:T(8,128)(2,1)S(1)}, u32[]{:S(2)}) %copy-start.7) | copy-done | bytes 2097176
  73.2 4.3 %all-to-all-start.2 = ((bf16[8,1024,128]{2,1,0:T(8,128)(2,1)}), bf16[8,1024,128]{2,1,0:T(8,128)(2,1)}, u32[]{:S(2)}, u32[]{:S(2)}) async-start(bf16[8,1024,128]{2,1,0:T(8,128)(2,1)} %copy-done), calls=%async_computation.2 | async-start | bytes 4194304 | tf_op jit(solution)/shard_map/all_to_all | solution.py:255
  77.6 1.6 %copy-done.4 = bf16[1024,1024]{1,0:T(8,128)(2,1)S(1)} copy-done((bf16[1024,1024]{1,0:T(8,128)(2,1)S(1)}, bf16[1024,1024]{1,0:T(8,128)(2,1)}, u32[]{:S(2)}) %copy-start.4) | copy-done | bytes 2097176
  79.2 1.1 turn.1.turned_ref
  80.3 1.3 %copy-done.5 = bf16[1024,1024]{1,0:T(8,128)(2,1)} copy-done((bf16[1024,1024]{1,0:T(8,128)(2,1)}, bf16[1024,1024]{1,0:T(8,128)(2,1)S(1)}, u32[]{:S(2)}) %copy-start.5) | copy-done | bytes 2097176
  81.6 4.8 %left_grads.1.left_ref = bf16[16,32,128]{2,1,0:T(8,128)(2,1)S(1)} custom-call(bf16[1024,1024]{1,0:T(8,128)(2,1)S(1)} %copy-done.8, bf16[8,1024,128]{2,1,0:T(8,128)(2,1)S(1)} %all-to-all-done.1.in_ref), custom_call_target="tpu_custom_call" | custom-call | flops 4294967296 | bytes 4194304 | tf_op jit(solution)/shard_map/left_grads/pallas_call | solution.py:192
  86.4 18.2 %all-to-all-done.2.in_ref = bf16[8,1024,128]{2,1,0:T(8,128)(2,1)} async-done(((bf16[8,1024,128]{2,1,0:T(8,128)(2,1)}), bf16[8,1024,128]{2,1,0:T(8,128)(2,1)}, u32[]{:S(2)}, u32[]{:S(2)}) %all-to-all-start.2) | async-done | bytes 2097184 | tf_op jit(solution)/shard_map/all_to_all | solution.py:255
  104.6 1.6 %copy-done.6 = bf16[1024,1024]{1,0:T(8,128)(2,1)S(1)} copy-done((bf16[1024,1024]{1,0:T(8,128)(2,1)S(1)}, bf16[1024,1024]{1,0:T(8,128)(2,1)}, u32[]{:S(2)}) %copy-start.6) | copy-done | bytes 2097176
  106.2 4.5 %right_grads.1 = bf16[16,96,128]{2,1,0:T(8,128)(2,1)S(1)} custom-call(bf16[8,1024,128]{2,1,0:T(8,128)(2,1)} %all-to-all-done.2.in_ref, bf16[1024,1024]{1,0:T(8,128)(2,1)S(1)} %copy-done.6, bf16[16,32,128]{2,1,0:T(8,128)(2,1)S(1)} %left_grads.1.left_ref), custom_call_target="tpu_custom_call" | custom-call | flops 2147483648 | bytes 4194304 | tf_op jit(solution)/shard_map/right_grads/pallas_call | solution.py:223
  110.7 18.1 %all_to_all.21 = bf16[16,96,128]{2,1,0:T(8,128)(2,1)S(1)} all-to-all(bf16[16,96,128]{2,1,0:T(8,128)(2,1)S(1)} %right_grads.1), channel_id=1, replica_groups=mesh['seq'=16,'blk'=8] {'seq'}, dimensions={0} | all-to-all | bytes 786432 | tf_op jit(solution)/shard_map/all_to_all | solution.py:258
  128.8 0.1 convert_reduce_fusion
  128.9 0.6 slice_bitcast_fusion
  129.5 0.1 reshape.24
  129.6 0.6 copy.8
  (16 shorter events, 0.0 us)
Async XLA Ops:
  21.1 1.6 %copy-start.3 = (bf16[1024,1024]{1,0:T(8,128)(2,1)S(1)}, bf16[1024,1024]{1,0:T(8,128)(2,1)}, u32[]{:S(2)}) copy-start(bf16[1024,1024]{1,0:T(8,128)(2,1)} %x_ref.3) | copy-start | bytes 6291460
  26.1 1.3 %copy-start.1 = (bf16[8,1024,128]{2,1,0:T(8,128)(2,1)}, bf16[8,1024,128]{2,1,0:T(8,128)(2,1)S(1)}, u32[]{:S(2)}) copy-start(bf16[8,1024,128]{2,1,0:T(8,128)(2,1)S(1)} %mix.1) | copy-start | bytes 6291460
  27.4 30.9 %all-to-all-start.1 = ((bf16[8,1024,128]{2,1,0:T(8,128)(2,1)}), bf16[8,1024,128]{2,1,0:T(8,128)(2,1)S(1)}, u32[]{:S(2)}, u32[]{:S(2)}) async-start(bf16[8,1024,128]{2,1,0:T(8,128)(2,1)} %copy-done.1), calls=%async_computation.1 | async-start | bytes 4194304 | tf_op jit(solution)/shard_map/all_to_all | solution.py:251
  33.6 1.3 %copy-start.9 = (bf16[1024,1024]{1,0:T(8,128)(2,1)}, bf16[1024,1024]{1,0:T(8,128)(2,1)S(1)}, u32[]{:S(2)}) copy-start(bf16[1024,1024]{1,0:T(8,128)(2,1)S(1)} %get-tuple-element.8.wide_ref) | copy-start | bytes 6291460
  34.9 1.3 %copy-start.11 = (bf16[1024,1024]{1,0:T(8,128)(2,1)}, bf16[1024,1024]{1,0:T(8,128)(2,1)S(1)}, u32[]{:S(2)}) copy-start(bf16[1024,1024]{1,0:T(8,128)(2,1)S(1)} %get-tuple-element.9.back_ref) | copy-start | bytes 6291460
  58.3 1.6 %copy-start.2 = (bf16[1024,1024]{1,0:T(8,128)(2,1)S(1)}, bf16[1024,1024]{1,0:T(8,128)(2,1)}, u32[]{:S(2)}) copy-start(bf16[1024,1024]{1,0:T(8,128)(2,1)} %target_ref.1) | copy-start | bytes 6291460
  59.9 1.6 %copy-start.10 = (bf16[1024,1024]{1,0:T(8,128)(2,1)S(1)}, bf16[1024,1024]{1,0:T(8,128)(2,1)}, u32[]{:S(2)}) copy-start(bf16[1024,1024]{1,0:T(8,128)(2,1)} %copy-done.9) | copy-start | bytes 6291460
  61.4 1.6 %copy-start.12 = (bf16[1024,1024]{1,0:T(8,128)(2,1)S(1)}, bf16[1024,1024]{1,0:T(8,128)(2,1)}, u32[]{:S(2)}) copy-start(bf16[1024,1024]{1,0:T(8,128)(2,1)} %copy-done.11) | copy-start | bytes 6291460
  70.6 1.3 %copy-start = (bf16[8,1024,128]{2,1,0:T(8,128)(2,1)}, bf16[8,1024,128]{2,1,0:T(8,128)(2,1)S(1)}, u32[]{:S(2)}) copy-start(bf16[8,1024,128]{2,1,0:T(8,128)(2,1)S(1)} %get-tuple-element.11) | copy-start | bytes 6291460
  71.9 1.4 %copy-start.7 = (bf16[1024,1024]{1,0:T(8,128)(2,1)}, bf16[1024,1024]{1,0:T(8,128)(2,1)S(1)}, u32[]{:S(2)}) copy-start(bf16[1024,1024]{1,0:T(8,128)(2,1)S(1)} %get-tuple-element.12.grad_ref) | copy-start | bytes 6291460
  73.2 31.4 %all-to-all-start.2 = ((bf16[8,1024,128]{2,1,0:T(8,128)(2,1)}), bf16[8,1024,128]{2,1,0:T(8,128)(2,1)}, u32[]{:S(2)}, u32[]{:S(2)}) async-start(bf16[8,1024,128]{2,1,0:T(8,128)(2,1)} %copy-done), calls=%async_computation.2 | async-start | bytes 4194304 | tf_op jit(solution)/shard_map/all_to_all | solution.py:255
  77.6 1.6 %copy-start.4 = (bf16[1024,1024]{1,0:T(8,128)(2,1)S(1)}, bf16[1024,1024]{1,0:T(8,128)(2,1)}, u32[]{:S(2)}) copy-start(bf16[1024,1024]{1,0:T(8,128)(2,1)} %x_ref.3) | copy-start | bytes 6291460
  79.2 2.5 %copy-start.8 = (bf16[1024,1024]{1,0:T(8,128)(2,1)S(1)}, bf16[1024,1024]{1,0:T(8,128)(2,1)}, u32[]{:S(2)}) copy-start(bf16[1024,1024]{1,0:T(8,128)(2,1)} %copy-done.7) | copy-start | bytes 6291460
  80.3 1.4 %copy-start.5 = (bf16[1024,1024]{1,0:T(8,128)(2,1)}, bf16[1024,1024]{1,0:T(8,128)(2,1)S(1)}, u32[]{:S(2)}) copy-start(bf16[1024,1024]{1,0:T(8,128)(2,1)S(1)} %turn.1.turned_ref) | copy-start | bytes 6291460
  104.6 1.6 %copy-start.6 = (bf16[1024,1024]{1,0:T(8,128)(2,1)S(1)}, bf16[1024,1024]{1,0:T(8,128)(2,1)}, u32[]{:S(2)}) copy-start(bf16[1024,1024]{1,0:T(8,128)(2,1)} %copy-done.5) | copy-start | bytes 6291460

commit v2 on v0

v2 whole, which is shorter than its diff:
```python
import functools
import math

import jax
import jax.numpy as jnp
from jax import lax
from jax.experimental import pallas as pl
from jax.experimental.pallas import tpu as pltpu
from jax.sharding import PartitionSpec as P

BF = jnp.bfloat16
F32 = jnp.float32
MIB = 1 << 20
ROOT = math.sqrt(2.0 / math.pi)
CUBE = 0.044715


def iota(shape, dim):
    return lax.broadcasted_iota(jnp.int32, shape, dim)


def dot(a, b, dims=((1,), (0,))):
    return lax.dot_general(a, b, (dims, ((), ())), preferred_element_type=F32)


def params(limit=24):
    return pltpu.CompilerParams(vmem_limit_bytes=limit * MIB)


def cost(flops, size):
    return pl.CostEstimate(flops=int(flops), bytes_accessed=int(size), transcendentals=0)


def parity():
    return lax.rem(lax.axis_index("blk"), 2)


def joined(parts):
    return jnp.concatenate(parts, axis=1)


def halves(blocks):
    low = iota(blocks[0].shape, 1) < 64
    first = joined([jnp.where(low, blocks[2 * p], blocks[2 * p + 1]) for p in range(4)])
    second = joined([jnp.where(low, blocks[2 * p + 1], blocks[2 * p]) for p in range(4)])
    return first, second


def split(blocks):
    even = ((iota(blocks[0].shape, 1) >> 5) & 1) == 0
    first = joined([jnp.where(even, blocks[2 * p], blocks[2 * p + 1]) for p in range(4)])
    second = joined([jnp.where(even, blocks[2 * p + 1], blocks[2 * p]) for p in range(4)])
    return first, second


def source(pair, g, kh, par):
    return 2 * (2 * pair + ((g & 1) ^ kh)) + ((g >> 1) ^ par)


def pack_kernel(right_ref, left_ref, out_ref):
    right = right_ref[...].astype(F32).reshape(64, 128)
    left = left_ref[...].astype(F32).reshape(64, 64)
    whole = jnp.concatenate([right, joined([left[:32], left[32:]])], axis=0).astype(BF)
    for s in range(16):
        out_ref[s] = whole


def pack(right, left):
    return pl.pallas_call(
        pack_kernel,
        out_shape=jax.ShapeDtypeStruct((16, 96, 128), BF),
        compiler_params=params(),
        name="pack",
    )(right, left)


def permutation():
    r, q = iota((512, 512), 0), iota((512, 512), 1)
    here = ((r >> 6) == ((q >> 2) & 7)) & (((r >> 2) & 15) == (q >> 5)) & ((r & 3) == (q & 3))
    return here.astype(F32).astype(BF)


def spread(h, par):
    r, f = iota((128, 512), 0), iota((128, 512), 1)
    device = ((f >> 7) << 1) + (((f >> 6) & 1) ^ h)
    k = (device << 3) + ((((f >> 5) & 1) ^ par) << 2) + ((f >> 3) & 3)
    return (r == k + h * 64).astype(F32).astype(BF)


def same_block(shape):
    return (iota(shape, 0) >> 6) == (iota(shape, 1) & 7)


def mix_kernel(x_ref, g_ref, out_ref, back_ref, big_ref):
    @pl.when(pl.program_id(0) == 0)
    def _():
        par = parity()
        lane_k = (iota((128, 512), 1) >> 3) & 3
        for kh in range(2):
            rows = [
                g_ref[source(p, g, kh, par), kh * 32 : kh * 32 + 32, :].astype(F32)
                for p in range(4)
                for g in range(4)
            ]
            turned = jnp.concatenate(rows, axis=0).T
            for k in range(4):
                big_ref[kh, k * 128 : (k + 1) * 128, :] = jnp.where(lane_k == k, turned, 0.0).astype(BF)
        packed = jnp.concatenate([g_ref[s, 64:96, :] for s in range(16)], axis=0)
        ordered = dot(permutation(), packed).astype(BF)
        for h in range(2):
            full = dot(ordered, spread(h, par))
            back_ref[h] = jnp.where(same_block((512, 512)), full, 0.0).astype(BF)

    first = dot(x_ref[:, :512], big_ref[0]).astype(BF)
    second = dot(x_ref[:, 512:], big_ref[1]).astype(BF)
    even = ((iota((first.shape[0], 128), 1) >> 5) & 1) == 0
    for p in range(4):
        lanes = slice(p * 128, (p + 1) * 128)
        a, b = first[:, lanes], second[:, lanes]
        out_ref[2 * p] = jnp.where(even, a, b)
        out_ref[2 * p + 1] = jnp.where(even, b, a)


def mix(x, gathered):
    rows = x.shape[0]
    step = 256
    return pl.pallas_call(
        mix_kernel,
        grid=(rows // step,),
        in_specs=[
            pl.BlockSpec((step, 1024), lambda t: (t, 0)),
            pl.BlockSpec((16, 96, 128), lambda t: (0, 0, 0)),
        ],
        out_specs=(
            pl.BlockSpec((8, step, 128), lambda t: (0, t, 0)),
            pl.BlockSpec((2, 512, 512), lambda t: (0, 0, 0)),
        ),
        out_shape=(
            jax.ShapeDtypeStruct((8, rows, 128), BF),
            jax.ShapeDtypeStruct((2, 512, 512), BF),
        ),
        scratch_shapes=[pltpu.VMEM((2, 512, 512), BF)],
        compiler_params=params(),
        cost_estimate=cost(rows * 1024 * 1024, 4 * rows * 1024),
        name="mix",
    )(x, gathered)


def middle_kernel(scale, in_ref, back_ref, target_ref, student_ref, grad_ref, out_ref):
    turned = halves([in_ref[j] for j in range(8)])
    outs = []
    for h in range(2):
        lanes = slice(h * 512, (h + 1) * 512)
        v = dot(turned[h], back_ref[h], ((1,), (1,)))
        square = v * v
        p = 0.5 + 0.5 * jnp.tanh(v * (ROOT + (ROOT * CUBE) * square))
        act = v * p
        slope = p + (act - act * p) * (2.0 * ROOT + (6.0 * ROOT * CUBE) * square)
        student_ref[:, lanes] = act.astype(BF)
        grad = ((act - target_ref[:, lanes].astype(F32)) * (slope * scale)).astype(BF)
        grad_ref[:, lanes] = grad
        outs.append(dot(grad, back_ref[h]).astype(BF))
    low = iota((outs[0].shape[0], 128), 1) < 64
    for p in range(4):
        lanes = slice(p * 128, (p + 1) * 128)
        a, b = outs[0][:, lanes], outs[1][:, lanes]
        out_ref[2 * p] = jnp.where(low, a, b)
        out_ref[2 * p + 1] = jnp.where(low, b, a)


def middle(received, back, target, scale):
    rows = target.shape[0]
    step = 256
    block = pl.BlockSpec((8, step, 128), lambda t: (0, t, 0))
    line = pl.BlockSpec((step, 1024), lambda t: (t, 0))
    whole = pl.BlockSpec((2, 512, 512), lambda t: (0, 0, 0))
    flat = jax.ShapeDtypeStruct((rows, 1024), BF)
    return pl.pallas_call(
        functools.partial(middle_kernel, scale),
        grid=(rows // step,),
        in_specs=[block, whole, line],
        out_specs=(line, line, block),
        out_shape=(flat, flat, jax.ShapeDtypeStruct((8, rows, 128), BF)),
        compiler_params=params(),
        cost_estimate=cost(2 * rows * 1024 * 1024, 10 * rows * 1024),
        name="middle",
    )(received, back, target)


def grads_kernel(grad_ref, in_ref, back_ref, x_ref, out_ref):
    par = parity()
    turned = halves([in_ref[j] for j in range(8)])
    total = jnp.zeros((512, 128), F32)
    for h in range(2):
        full = dot(grad_ref[:, h * 512 : (h + 1) * 512], turned[h], ((0,), (0,)))
        full = jnp.where(same_block((512, 512)), full, 0.0).astype(BF)
        total = total + dot(full, spread(h, par), ((1,), (1,)))
    ordered = dot(permutation(), total.astype(BF), ((0,), (0,))).astype(BF)
    for s in range(16):
        out_ref[s, 64:96, :] = ordered[s * 32 : (s + 1) * 32, :]

    returned = split([back_ref[j] for j in range(8)])
    lane_k = (iota((128, 512), 1) >> 3) & 3
    for kh in range(2):
        full = dot(x_ref[:, kh * 512 : (kh + 1) * 512], returned[kh], ((0,), (0,)))
        kept = jnp.zeros((128, 512), F32)
        for k in range(4):
            kept = jnp.where(lane_k == k, full[k * 128 : (k + 1) * 128, :], kept)
        kept = kept.T.astype(BF)
        for p in range(4):
            for g in range(4):
                n = (p * 4 + g) * 32
                out_ref[source(p, g, kh, par), kh * 32 : kh * 32 + 32, :] = kept[n : n + 32, :]


def grads(grad, received, returned, x):
    rows = grad.shape[0]
    return pl.pallas_call(
        grads_kernel,
        out_shape=jax.ShapeDtypeStruct((16, 96, 128), BF),
        compiler_params=params(),
        cost_estimate=cost(2 * rows * 1024 * 1024, 8 * rows * 1024),
        name="grads",
    )(grad, received, returned, x)


def sum_kernel(in_ref, right_ref, left_ref):
    total = in_ref[0].astype(F32)
    for s in range(1, 16):
        total = total + in_ref[s].astype(F32)
    right_ref[...] = total[:64].reshape(8, 8, 128)
    left = total[64:]
    left_ref[:8] = left[:, :64].reshape(8, 4, 64)
    left_ref[8:] = left[:, 64:].reshape(8, 4, 64)


def sums(terms):
    return pl.pallas_call(
        sum_kernel,
        out_shape=(
            jax.ShapeDtypeStruct((8, 8, 128), F32),
            jax.ShapeDtypeStruct((16, 4, 64), F32),
        ),
        compiler_params=params(),
        name="sums",
    )(terms)


def shards(tokens, right_factor, left_factor, target):
    rows = tokens.shape[0]
    scale = 1.0 / math.sqrt(rows * lax.axis_size("seq"))
    gathered = lax.all_to_all(pack(right_factor, left_factor), "seq", 0, 0, tiled=True)
    mixed, back = mix(tokens, gathered)
    received = lax.all_to_all(mixed, "blk", 0, 0, tiled=True)
    student, grad, out = middle(received, back, target, scale)
    returned = lax.all_to_all(out, "blk", 0, 0, tiled=True)
    terms = grads(grad, received, returned, tokens)
    terms = lax.all_to_all(terms, "seq", 0, 0, tiled=True)
    right_grad, left_grad = sums(terms)
    return (student, right_grad, left_grad)


def solution(mesh):
    return jax.shard_map(
        shards,
        mesh=mesh,
        in_specs=(P("seq", "blk"), P("blk", "seq", None), P("blk", "seq", None), P("seq", "blk")),
        out_specs=(P("seq", "blk"), P("blk", "seq", None), P("blk", "seq", None)),
        check_vma=False,
    )
```

time: 281 us -> 112 us (0.40)
  waiting for transfers between devices: 159 us -> 0 us
  blocking collectives: 59 us -> 94 us
  starting transfers between devices: 15.9 us -> 0 us
  matrix products: 13.8 us -> 0 us
  between operations: 14.1 us -> 0.67 us
  Pallas kernels: 0 us -> 13.4 us
  local copies, waits for them, and re-layouts: 15.4 us -> 3.03 us
    psum x1 -> x0, waiting for transfers between devices: 135 us -> none  [shards(): lax.psum(right_term.astype(jnp.bfloat16), 'seq').astype(jnp.float32)]
    all_to_all x0 -> x4, blocking collectives: none -> 94 us  [the longest x1 30.8 us: shards(): received = lax.all_to_all(mixed, 'blk', 0, 0, tiled=True)]
    all_gather x2 -> x0, blocking collectives: 59 us -> none  [the longest x1 31.9 us: shards(): lax.all_gather(left_factor, 'seq', axis=1, tiled=True)]
    all_to_all x2 -> x0, waiting for transfers between devices: 23.8 us -> none  [the longest x1 23.8 us: shards(): lax.all_to_all(turned_grad, 'blk', split_axis=1, concat_axis=2, tiled=True)]
    all_to_all x2 -> x0, starting transfers between devices: 15.9 us -> none  [the longest x1 11.3 us: shards(): lax.all_to_all(turned_grad, 'blk', split_axis=1, concat_axis=2, tiled=True)]
    dot_general x5 -> x0, matrix products: 13.8 us -> none  [the longest x1 7.07 us: shards(): jnp.einsum('tkc,cmk->tcm', turned, left_full, preferred_element_type=jnp....]
    pallas_call x0 -> x5, Pallas kernels: none -> 13.4 us  [the longest x1 6.38 us: middle(): pl.pallas_call(functools.partial(middle_kernel, scale), grid=(rows // ste...]
    convert_element_type x3 -> x0, local copies, waits for them, and re-layouts: 9.08 us -> none  [the longest x1 4.14 us: shards(): target.reshape(rows, local_cols, nblocks).astype(jnp.float32)]
  transfers between devices with their start and end apart: 3 -> 0, of which waited for: 2 -> 0; matrix products, arithmetic and copies ran while one was open for 4% -> 0% of each run, Pallas kernels for 0% -> 0%
where the time goes in v2:
time: 112 us; the launch traced here: 111 us
  blocking collectives  94 us (84%)
  Pallas kernels  13.4 us (12%)
  local copies, waits for them, and re-layouts  3.03 us (3%)
    all_to_all x1, blocking collectives, shards(): received = lax.all_to_all(mixed, 'blk', 0, 0, tiled=True)  30.8 us
    all_to_all x1, blocking collectives, shards(): returned = lax.all_to_all(out, 'blk', 0, 0, tiled=True)  28.3 us
    all_to_all x1, blocking collectives, shards(): lax.all_to_all(pack(right_factor, left_factor), 'seq', 0, 0, tiled=True)  18.9 us
    all_to_all x1, blocking collectives, shards(): terms = lax.all_to_all(terms, 'seq', 0, 0, tiled=True)  16.1 us
    pallas_call x1, Pallas kernels, middle(): pl.pallas_call(functools.partial(middle_kernel, scale), grid=(rows // ste...  6.38 us
    pallas_call x1, Pallas kernels, grads(): pl.pallas_call(grads_kernel, out_shape=jax.ShapeDtypeStruct((16, 96, 128)...  3.37 us
    unnamed x10, local copies, waits for them, and re-layouts  3.03 us
    pallas_call x1, Pallas kernels, mix(): pl.pallas_call(mix_kernel, grid=(rows // step,), in_specs=[pl.BlockSpec((...  2.89 us

profile of v2, /device:TPU:0, one launch (start us, length us, event | category | flops | bytes accessed | tf_op | source)
XLA Modules:
  0.0 111.2 jit_solution(2663001693403302630)
XLA Ops:
  0.6 0.0 copy-start.2
  0.6 0.7 copy-done.2
  1.3 0.0 copy-start.3
  1.4 0.7 copy-done.3
  2.1 0.1 pack.1
  2.2 18.9 %all_to_all.20.g_ref = bf16[16,96,128]{2,1,0:T(8,128)(2,1)S(1)} all-to-all(bf16[16,96,128]{2,1,0:T(8,128)(2,1)S(1)} %pack.1), channel_id=1, replica_groups=mesh['seq'=16,'blk'=8] {'seq'}, dimensions={0} | all-to-all | bytes 786432 | tf_op jit(solution)/shard_map/all_to_all | solution.py:252
  21.0 0.0 copy-start
  21.0 1.6 %copy-done = bf16[1024,1024]{1,0:T(8,128)(2,1)S(1)} copy-done((bf16[1024,1024]{1,0:T(8,128)(2,1)S(1)}, bf16[1024,1024]{1,0:T(8,128)(2,1)}, u32[]{:S(2)}) %copy-start) | copy-done | bytes 2097176
  22.6 2.9 %mix.1 = (bf16[8,1024,128]{2,1,0:T(8,128)(2,1)S(1)}, bf16[2,512,512]{2,1,0:T(8,128)(2,1)S(1)}) custom-call(bf16[1024,1024]{1,0:T(8,128)(2,1)S(1)} %copy-done, bf16[16,96,128]{2,1,0:T(8,128)(2,1)S(1)} %all_to_all.20.g_ref), custom_call_target="tpu_custom_call" | custom-call | flops 1073741824 | bytes 4194304 | tf_op jit(solution)/shard_map/mix/pallas_call | solution.py:127
  25.5 0.0 copy-start.4
  25.6 30.8 %all_to_all.21.in_ref = bf16[8,1024,128]{2,1,0:T(8,128)(2,1)S(1)} all-to-all(bf16[8,1024,128]{2,1,0:T(8,128)(2,1)S(1)} %get-tuple-element.10), channel_id=1, replica_groups=mesh['seq'=16,'blk'=8] {'blk'}, dimensions={0} | all-to-all | bytes 4194304 | tf_op jit(solution)/shard_map/all_to_all | solution.py:254
  56.3 0.0 copy-done.4
  56.3 6.4 %middle.1 = (bf16[1024,1024]{1,0:T(8,128)(2,1)}, bf16[1024,1024]{1,0:T(8,128)(2,1)S(1)}, bf16[8,1024,128]{2,1,0:T(8,128)(2,1)S(1)}) custom-call(bf16[8,1024,128]{2,1,0:T(8,128)(2,1)S(1)} %all_to_all.21.in_ref, bf16[2,512,512]{2,1,0:T(8,128)(2,1)S(1)} %get-tuple-element.11.back_ref, bf16[1024,1024]{1,0:T(8,128)(2,1)S(1)} %copy-done.4), custom_call_target="tpu_custom_call" | custom-call | flops 2147483648 | bytes 10485760 | tf_op jit(solution)/shard_map/middle/pallas_call | solution.py:178
  62.7 0.0 copy-start.1
  62.7 28.3 %all_to_all.22.back_ref = bf16[8,1024,128]{2,1,0:T(8,128)(2,1)S(1)} all-to-all(bf16[8,1024,128]{2,1,0:T(8,128)(2,1)S(1)} %get-tuple-element.14), channel_id=1, replica_groups=mesh['seq'=16,'blk'=8] {'blk'}, dimensions={0} | all-to-all | bytes 4194304 | tf_op jit(solution)/shard_map/all_to_all | solution.py:256
  91.0 0.0 copy-done.1
  91.0 3.4 %grads.1 = bf16[16,96,128]{2,1,0:T(8,128)(2,1)S(1)} custom-call(bf16[1024,1024]{1,0:T(8,128)(2,1)S(1)} %get-tuple-element.13.grad_ref, bf16[8,1024,128]{2,1,0:T(8,128)(2,1)S(1)} %all_to_all.21.in_ref, bf16[8,1024,128]{2,1,0:T(8,128)(2,1)S(1)} %all_to_all.22.back_ref, bf16[1024,1024]{1,0:T(8,128)(2,1)S(1)} %copy-done.1), custom_call_target="tpu_custom_call" | custom-call | flops 2147483648 | bytes 8388608 | tf_op jit(solution)/shard_map/grads/pallas_call | solution.py:218
  94.4 16.1 %all_to_all.23.in_ref = bf16[16,96,128]{2,1,0:T(8,128)(2,1)S(1)} all-to-all(bf16[16,96,128]{2,1,0:T(8,128)(2,1)S(1)} %grads.1), channel_id=1, replica_groups=mesh['seq'=16,'blk'=8] {'seq'}, dimensions={0} | all-to-all | bytes 786432 | tf_op jit(solution)/shard_map/all_to_all | solution.py:258
  110.4 0.7 sums.1
Async XLA Ops:
  0.6 0.7 copy-start.2
  1.3 0.7 copy-start.3
  21.0 1.6 %copy-start = (bf16[1024,1024]{1,0:T(8,128)(2,1)S(1)}, bf16[1024,1024]{1,0:T(8,128)(2,1)}, u32[]{:S(2)}) copy-start(bf16[1024,1024]{1,0:T(8,128)(2,1)} %x_ref.3) | copy-start | bytes 6291460
  25.5 30.8 %copy-start.4 = (bf16[1024,1024]{1,0:T(8,128)(2,1)S(1)}, bf16[1024,1024]{1,0:T(8,128)(2,1)}, u32[]{:S(2)}) copy-start(bf16[1024,1024]{1,0:T(8,128)(2,1)} %target_ref.1) | copy-start | bytes 6291460
  62.7 28.3 %copy-start.1 = (bf16[1024,1024]{1,0:T(8,128)(2,1)S(1)}, bf16[1024,1024]{1,0:T(8,128)(2,1)}, u32[]{:S(2)}) copy-start(bf16[1024,1024]{1,0:T(8,128)(2,1)} %x_ref.3) | copy-start | bytes 6291460

commit v3 on v2

v3 whole, which is shorter than its diff:
```python
import functools
import math

import jax
import jax.numpy as jnp
from jax import lax
from jax.experimental import pallas as pl
from jax.experimental.pallas import tpu as pltpu
from jax.sharding import PartitionSpec as P

BF = jnp.bfloat16
F32 = jnp.float32
MIB = 1 << 20
ROOT = math.sqrt(2.0 / math.pi)
CUBE = 0.044715


def iota(shape, dim):
    return lax.broadcasted_iota(jnp.int32, shape, dim)


def dot(a, b, dims=((1,), (0,))):
    return lax.dot_general(a, b, (dims, ((), ())), preferred_element_type=F32)


def params(limit=24):
    return pltpu.CompilerParams(vmem_limit_bytes=limit * MIB)


def cost(flops, size):
    return pl.CostEstimate(flops=int(flops), bytes_accessed=int(size), transcendentals=0)


def in_hbm(x):
    return pltpu.with_memory_space_constraint(x, pltpu.HBM)


def parity():
    return lax.rem(lax.axis_index("blk"), 2)


def joined(parts):
    return jnp.concatenate(parts, axis=1)


def halves(blocks):
    low = iota(blocks[0].shape, 1) < 64
    first = joined([jnp.where(low, blocks[2 * p], blocks[2 * p + 1]) for p in range(4)])
    second = joined([jnp.where(low, blocks[2 * p + 1], blocks[2 * p]) for p in range(4)])
    return first, second


def split(blocks):
    even = ((iota(blocks[0].shape, 1) >> 5) & 1) == 0
    first = joined([jnp.where(even, blocks[2 * p], blocks[2 * p + 1]) for p in range(4)])
    second = joined([jnp.where(even, blocks[2 * p + 1], blocks[2 * p]) for p in range(4)])
    return first, second


def source(pair, g, kh, par):
    return 2 * (2 * pair + ((g & 1) ^ kh)) + ((g >> 1) ^ par)


def pack_kernel(right_hbm, left_hbm, out_ref, right_ref, left_ref, sems):
    copies = [
        pltpu.make_async_copy(right_hbm, right_ref, sems.at[0]),
        pltpu.make_async_copy(left_hbm, left_ref, sems.at[1]),
    ]
    for copy in copies:
        copy.start()
    for copy in copies:
        copy.wait()
    right = right_ref[...].astype(F32).reshape(64, 128)
    left = left_ref[...].astype(F32).reshape(64, 64)
    whole = jnp.concatenate([right, joined([left[:32], left[32:]])], axis=0).astype(BF)
    for s in range(16):
        out_ref[s] = whole


def pack(right, left):
    return pl.pallas_call(
        pack_kernel,
        in_specs=[pl.BlockSpec(memory_space=pltpu.HBM)] * 2,
        out_shape=jax.ShapeDtypeStruct((16, 96, 128), BF),
        scratch_shapes=[
            pltpu.VMEM(right.shape, BF),
            pltpu.VMEM(left.shape, BF),
            pltpu.SemaphoreType.DMA((2,)),
        ],
        compiler_params=params(),
        name="pack",
    )(in_hbm(right), in_hbm(left))


def exchange(x, a, b):
    low = iota((8, x.shape[1]), 0) < 4

    def tile(i, j):
        n = (i * b + j) * 4
        return x[n : n + 8]

    parts = []
    for j in range(0, b, 2):
        pairs = [(tile(i, j), tile(i + 1, j)) for i in range(0, a, 2)]
        parts += [jnp.where(low, u, pltpu.roll(v, 4, 0)) for u, v in pairs]
        parts += [jnp.where(low, pltpu.roll(u, 4, 0), v) for u, v in pairs]
    return jnp.concatenate(parts, axis=0)


def spread(h, par):
    r, f = iota((128, 512), 0), iota((128, 512), 1)
    device = ((f >> 7) << 1) + (((f >> 6) & 1) ^ h)
    k = (device << 3) + ((((f >> 5) & 1) ^ par) << 2) + ((f >> 3) & 3)
    return (r == k + h * 64).astype(F32).astype(BF)


def same_block(shape):
    return (iota(shape, 0) >> 6) == (iota(shape, 1) & 7)


def mix_kernel(x_hbm, g_ref, out_ref, back_ref, x_ref, sems):
    copies = []
    for kh in range(2):
        lanes = slice(kh * 512, (kh + 1) * 512)
        copies.append(pltpu.make_async_copy(x_hbm.at[:, lanes], x_ref.at[kh], sems.at[kh]))
        copies[kh].start()
    par = parity()
    packed = jnp.concatenate([g_ref[s, 64:96, :].astype(F32) for s in range(16)], axis=0)
    ordered = exchange(packed, 16, 8).astype(BF)
    for h in range(2):
        full = dot(ordered, spread(h, par))
        back_ref[h] = jnp.where(same_block((512, 512)), full, 0.0).astype(BF)
    lane_k = (iota((128, 512), 1) >> 3) & 3
    mixed = []
    for kh in range(2):
        rows = [
            g_ref[source(p, g, kh, par), kh * 32 : kh * 32 + 32, :].astype(F32)
            for p in range(4)
            for g in range(4)
        ]
        turned = jnp.concatenate(rows, axis=0).T
        big = jnp.concatenate([jnp.where(lane_k == k, turned, 0.0) for k in range(4)], axis=0)
        copies[kh].wait()
        mixed.append(dot(x_ref[kh], big.astype(BF)).astype(BF))
    even = ((iota((mixed[0].shape[0], 128), 1) >> 5) & 1) == 0
    for p in range(4):
        lanes = slice(p * 128, (p + 1) * 128)
        a, b = mixed[0][:, lanes], mixed[1][:, lanes]
        out_ref[2 * p] = jnp.where(even, a, b)
        out_ref[2 * p + 1] = jnp.where(even, b, a)


def mix(x, gathered):
    rows = x.shape[0]
    return pl.pallas_call(
        mix_kernel,
        out_shape=(
            jax.ShapeDtypeStruct((8, rows, 128), BF),
            jax.ShapeDtypeStruct((2, 512, 512), BF),
        ),
        in_specs=[pl.BlockSpec(memory_space=pltpu.HBM), pl.BlockSpec()],
        scratch_shapes=[pltpu.VMEM((2, rows, 512), BF), pltpu.SemaphoreType.DMA((2,))],
        compiler_params=params(),
        cost_estimate=cost(rows * 1024 * 1024, 4 * rows * 1024),
        name="mix",
    )(in_hbm(x), gathered)


def middle_kernel(in_ref, back_ref, target_ref, student_ref, left_ref, out_ref):
    par = parity()
    total = jnp.zeros((512, 128), F32)
    turned = halves([in_ref[j] for j in range(8)])
    outs = []
    for h in range(2):
        lanes = slice(h * 512, (h + 1) * 512)
        v = dot(turned[h], back_ref[h], ((1,), (1,)))
        square = v * v
        p = 0.5 + 0.5 * jnp.tanh(v * (ROOT + (ROOT * CUBE) * square))
        act = v * p
        slope = p + (act - act * p) * (2.0 * ROOT + (6.0 * ROOT * CUBE) * square)
        student_ref[:, lanes] = act.astype(BF)
        grad = ((act - target_ref[:, lanes].astype(F32)) * slope).astype(BF)
        outs.append(dot(grad, back_ref[h]).astype(BF))
        full = dot(grad, turned[h], ((0,), (0,)))
        full = jnp.where(same_block((512, 512)), full, 0.0).astype(BF)
        total = total + dot(full, spread(h, par), ((1,), (1,)))
    low = iota((outs[0].shape[0], 128), 1) < 64
    for p in range(4):
        lanes = slice(p * 128, (p + 1) * 128)
        a, b = outs[0][:, lanes], outs[1][:, lanes]
        out_ref[2 * p] = jnp.where(low, a, b)
        out_ref[2 * p + 1] = jnp.where(low, b, a)
    ordered = exchange(total, 8, 16).astype(BF)
    for s in range(16):
        left_ref[s] = ordered[s * 32 : (s + 1) * 32, :]


def middle(received, back, target):
    rows = target.shape[0]
    return pl.pallas_call(
        middle_kernel,
        out_shape=(
            pltpu.VMEM((rows, 1024), BF),
            jax.ShapeDtypeStruct((16, 32, 128), BF),
            jax.ShapeDtypeStruct((8, rows, 128), BF),
        ),
        compiler_params=params(),
        cost_estimate=cost(2 * rows * 1024 * 1024, 10 * rows * 1024),
        name="middle",
    )(received, back, target)


def grads_kernel(student_ref, left_ref, back_ref, x_ref, student_hbm, out_ref, sem):
    copy = pltpu.make_async_copy(student_ref, student_hbm, sem)
    copy.start()
    par = parity()
    returned = split([back_ref[j] for j in range(8)])
    row_k = (iota((512, 128), 0) >> 3) & 3
    for kh in range(2):
        full = dot(returned[kh], x_ref[:, kh * 512 : (kh + 1) * 512], ((0,), (0,)))
        kept = jnp.zeros((512, 128), F32)
        for k in range(4):
            kept = jnp.where(row_k == k, full[:, k * 128 : (k + 1) * 128], kept)
        kept = kept.astype(BF)
        for p in range(4):
            for g in range(4):
                n = (p * 4 + g) * 32
                out_ref[source(p, g, kh, par), kh * 32 : kh * 32 + 32, :] = kept[n : n + 32, :]
    for s in range(16):
        out_ref[s, 64:96, :] = left_ref[s]
    copy.wait()


def grads(student, left, returned, x):
    rows = x.shape[0]
    return pl.pallas_call(
        grads_kernel,
        out_shape=(
            pltpu.HBM(student.shape, BF),
            jax.ShapeDtypeStruct((16, 96, 128), BF),
        ),
        out_specs=(pl.BlockSpec(memory_space=pltpu.HBM), pl.BlockSpec()),
        scratch_shapes=[pltpu.SemaphoreType.DMA],
        compiler_params=params(),
        cost_estimate=cost(2 * rows * 1024 * 1024, 8 * rows * 1024),
        name="grads",
    )(student, left, returned, x)


def sum_kernel(scale, in_ref, right_ref, left_ref):
    total = in_ref[0].astype(F32)
    for s in range(1, 16):
        total = total + in_ref[s].astype(F32)
    total = total * scale
    right_ref[...] = total[:64].reshape(8, 8, 128)
    left = total[64:]
    left_ref[:8] = left[:, :64].reshape(8, 4, 64)
    left_ref[8:] = left[:, 64:].reshape(8, 4, 64)


def sums(terms, scale):
    return pl.pallas_call(
        functools.partial(sum_kernel, scale),
        out_shape=(
            jax.ShapeDtypeStruct((8, 8, 128), F32),
            jax.ShapeDtypeStruct((16, 4, 64), F32),
        ),
        compiler_params=params(),
        name="sums",
    )(terms)


def shards(tokens, right_factor, left_factor, target):
    rows = tokens.shape[0]
    scale = 1.0 / math.sqrt(rows * lax.axis_size("seq"))
    gathered = lax.all_to_all(pack(right_factor, left_factor), "seq", 0, 0, tiled=True)
    mixed, back = mix(tokens, gathered)
    received = lax.all_to_all(mixed, "blk", 0, 0, tiled=True)
    student, left, out = middle(received, back, target)
    returned = lax.all_to_all(out, "blk", 0, 0, tiled=True)
    student, terms = grads(student, left, returned, tokens)
    terms = lax.all_to_all(terms, "seq", 0, 0, tiled=True)
    right_grad, left_grad = sums(terms, scale)
    return (student, right_grad, left_grad)


def solution(mesh):
    return jax.shard_map(
        shards,
        mesh=mesh,
        in_specs=(P("seq", "blk"), P("blk", "seq", None), P("blk", "seq", None), P("seq", "blk")),
        out_specs=(P("seq", "blk"), P("blk", "seq", None), P("blk", "seq", None)),
        check_vma=False,
    )
```

time: 112 us -> 106 us (0.946)
  local copies, waits for them, and re-layouts: 3.03 us -> 0.01 us
  Pallas kernels: 13.4 us -> 11 us
    unnamed x10 -> x4, local copies, waits for them, and re-layouts: 3.03 us -> 0.01 us
    pallas_call x5, Pallas kernels: 13.4 us -> 11 us  [the longest x1 5.4 us: middle(): pl.pallas_call(middle_kernel, out_shape=(pltpu.VMEM((rows, 1024), BF), ja...]
where the time goes in v3:
time: 106 us
  blocking collectives  94 us (89%)
  Pallas kernels  11 us (10%)
    all_to_all x1, blocking collectives, shards(): received = lax.all_to_all(mixed, 'blk', 0, 0, tiled=True)  30.8 us
    all_to_all x1, blocking collectives, shards(): returned = lax.all_to_all(out, 'blk', 0, 0, tiled=True)  28.3 us
    all_to_all x1, blocking collectives, shards(): lax.all_to_all(pack(right_factor, left_factor), 'seq', 0, 0, tiled=True)  18.9 us
    all_to_all x1, blocking collectives, shards(): terms = lax.all_to_all(terms, 'seq', 0, 0, tiled=True)  16.1 us
    pallas_call x1, Pallas kernels, middle(): pl.pallas_call(middle_kernel, out_shape=(pltpu.VMEM((rows, 1024), BF), ja...  5.4 us
    pallas_call x1, Pallas kernels, mix(): pl.pallas_call(mix_kernel, out_shape=(jax.ShapeDtypeStruct((8, rows, 128)...  2.7 us

profile of v3, /device:TPU:0, one launch (start us, length us, event | category | flops | bytes accessed | tf_op | source)
XLA Modules:
  0.0 105.7 jit_solution(17838769498412886514)
XLA Ops:
  0.6 0.8 pack.1
  1.5 18.9 %all_to_all.20.g_ref = bf16[16,96,128]{2,1,0:T(8,128)(2,1)S(1)} all-to-all(bf16[16,96,128]{2,1,0:T(8,128)(2,1)S(1)} %pack.1), channel_id=1, replica_groups=mesh['seq'=16,'blk'=8] {'seq'}, dimensions={0} | all-to-all | bytes 786432 | tf_op jit(solution)/shard_map/all_to_all | solution.py:276
  20.4 2.7 %mix.1 = (bf16[8,1024,128]{2,1,0:T(8,128)(2,1)S(1)}, bf16[2,512,512]{2,1,0:T(8,128)(2,1)S(1)}) custom-call(bf16[1024,1024]{1,0:T(8,128)(2,1)} %x_ref.1, bf16[16,96,128]{2,1,0:T(8,128)(2,1)S(1)} %all_to_all.20.g_ref), custom_call_target="tpu_custom_call" | custom-call | flops 1073741824 | bytes 4194304 | tf_op jit(solution)/shard_map/mix/pallas_call | solution.py:155
  23.1 0.0 copy-start
  23.1 30.8 %all_to_all.21.in_ref = bf16[8,1024,128]{2,1,0:T(8,128)(2,1)S(1)} all-to-all(bf16[8,1024,128]{2,1,0:T(8,128)(2,1)S(1)} %get-tuple-element.12), channel_id=1, replica_groups=mesh['seq'=16,'blk'=8] {'blk'}, dimensions={0} | all-to-all | bytes 4194304 | tf_op jit(solution)/shard_map/all_to_all | solution.py:278
  53.9 0.0 copy-done
  53.9 5.4 %middle.1 = (bf16[1024,1024]{1,0:T(8,128)(2,1)S(1)}, bf16[16,32,128]{2,1,0:T(8,128)(2,1)S(1)}, bf16[8,1024,128]{2,1,0:T(8,128)(2,1)S(1)}) custom-call(bf16[8,1024,128]{2,1,0:T(8,128)(2,1)S(1)} %all_to_all.21.in_ref, bf16[2,512,512]{2,1,0:T(8,128)(2,1)S(1)} %get-tuple-element.13.back_ref, bf16[1024,1024]{1,0:T(8,128)(2,1)S(1)} %copy-done), custom_call_target="tpu_custom_call" | custom-call | flops 2147483648 | bytes 10485760 | tf_op jit(solution)/shard_map/middle/pallas_call | solution.py:200
  59.3 0.0 copy-start.1
  59.3 28.3 %all_to_all.22.back_ref = bf16[8,1024,128]{2,1,0:T(8,128)(2,1)S(1)} all-to-all(bf16[8,1024,128]{2,1,0:T(8,128)(2,1)S(1)} %get-tuple-element.16), channel_id=1, replica_groups=mesh['seq'=16,'blk'=8] {'blk'}, dimensions={0} | all-to-all | bytes 4194304 | tf_op jit(solution)/shard_map/all_to_all | solution.py:280
  87.6 0.0 copy-done.1
  87.6 1.3 %grads.1 = (bf16[1024,1024]{1,0:T(8,128)(2,1)}, bf16[16,96,128]{2,1,0:T(8,128)(2,1)S(1)}) custom-call(bf16[1024,1024]{1,0:T(8,128)(2,1)S(1)} %get-tuple-element.14.student_ref, bf16[16,32,128]{2,1,0:T(8,128)(2,1)S(1)} %get-tuple-element.15.left_ref, bf16[8,1024,128]{2,1,0:T(8,128)(2,1)S(1)} %all_to_all.22.back_ref, bf16[1024,1024]{1,0:T(8,128)(2,1)S(1)} %copy-done.1), custom_call_target="tpu_custom_call" | custom-call | flops 2147483648 | bytes 8388608 | tf_op jit(solution)/shard_map/grads/pallas_call | solution.py:236
  88.9 16.1 %all_to_all.23.in_ref = bf16[16,96,128]{2,1,0:T(8,128)(2,1)S(1)} all-to-all(bf16[16,96,128]{2,1,0:T(8,128)(2,1)S(1)} %get-tuple-element.18), channel_id=1, replica_groups=mesh['seq'=16,'blk'=8] {'seq'}, dimensions={0} | all-to-all | bytes 786432 | tf_op jit(solution)/shard_map/all_to_all | solution.py:282
  105.0 0.7 sums.1
Async XLA Ops:
  23.1 30.8 %copy-start = (bf16[1024,1024]{1,0:T(8,128)(2,1)S(1)}, bf16[1024,1024]{1,0:T(8,128)(2,1)}, u32[]{:S(2)}) copy-start(bf16[1024,1024]{1,0:T(8,128)(2,1)} %target_ref.1) | copy-start | bytes 6291460
  59.3 28.3 %copy-start.1 = (bf16[1024,1024]{1,0:T(8,128)(2,1)S(1)}, bf16[1024,1024]{1,0:T(8,128)(2,1)}, u32[]{:S(2)}) copy-start(bf16[1024,1024]{1,0:T(8,128)(2,1)} %x_ref.1) | copy-start | bytes 6291460

commit v4 on v3

--- a/solution.py
+++ b/solution.py
@@ -57,8 +57,16 @@
     return first, second
 
 
-def source(pair, g, kh, par):
-    return 2 * (2 * pair + ((g & 1) ^ kh)) + ((g >> 1) ^ par)
+def chip(pair, g, kh):
+    return 2 * pair + ((g & 1) ^ kh)
+
+
+def core():
+    return lax.rem(lax.axis_index("seq"), 2)
+
+
+def flip():
+    return lax.rem(lax.axis_index("seq") + lax.axis_index("blk"), 2)
 
 
 def pack_kernel(right_hbm, left_hbm, out_ref, right_ref, left_ref, sems):
@@ -73,7 +81,7 @@
     right = right_ref[...].astype(F32).reshape(64, 128)
     left = left_ref[...].astype(F32).reshape(64, 64)
     whole = jnp.concatenate([right, joined([left[:32], left[32:]])], axis=0).astype(BF)
-    for s in range(16):
+    for s in range(8):
         out_ref[s] = whole
 
 
@@ -81,7 +89,7 @@
     return pl.pallas_call(
         pack_kernel,
         in_specs=[pl.BlockSpec(memory_space=pltpu.HBM)] * 2,
-        out_shape=jax.ShapeDtypeStruct((16, 96, 128), BF),
+        out_shape=jax.ShapeDtypeStruct((8, 96, 128), BF),
         scratch_shapes=[
             pltpu.VMEM(right.shape, BF),
             pltpu.VMEM(left.shape, BF),
@@ -118,14 +126,32 @@
     return (iota(shape, 0) >> 6) == (iota(shape, 1) & 7)
 
 
-def mix_kernel(x_hbm, g_ref, out_ref, back_ref, x_ref, sems):
-    copies = []
-    for kh in range(2):
-        lanes = slice(kh * 512, (kh + 1) * 512)
-        copies.append(pltpu.make_async_copy(x_hbm.at[:, lanes], x_ref.at[kh], sems.at[kh]))
-        copies[kh].start()
+def fetch_kernel(x_hbm, after_ref, out_ref, sem):
+    copy = pltpu.make_async_copy(x_hbm, out_ref, sem)
+    copy.start()
+    copy.wait()
+
+
+def fetch(x, after):
+    return pl.pallas_call(
+        fetch_kernel,
+        in_specs=[pl.BlockSpec(memory_space=pltpu.HBM), pl.BlockSpec()],
+        out_shape=pltpu.VMEM(x.shape, BF),
+        scratch_shapes=[pltpu.SemaphoreType.DMA],
+        compiler_params=params(8),
+        cost_estimate=cost(0, 8 * MIB),
+        name="fetch",
+    )(in_hbm(x), after)
+
+
+def mix_kernel(x_ref, own_ref, sib_ref, out_ref, back_ref):
     par = parity()
-    packed = jnp.concatenate([g_ref[s, 64:96, :].astype(F32) for s in range(16)], axis=0)
+    first = core() == 0
+    rows = []
+    for n in range(8):
+        own, sib = own_ref[n, 64:96, :].astype(F32), sib_ref[n, 64:96, :].astype(F32)
+        rows += [jnp.where(first, own, sib), jnp.where(first, sib, own)]
+    packed = jnp.concatenate(rows, axis=0)
     ordered = exchange(packed, 16, 8).astype(BF)
     for h in range(2):
         full = dot(ordered, spread(h, par))
@@ -133,15 +159,15 @@
     lane_k = (iota((128, 512), 1) >> 3) & 3
     mixed = []
     for kh in range(2):
-        rows = [
-            g_ref[source(p, g, kh, par), kh * 32 : kh * 32 + 32, :].astype(F32)
-            for p in range(4)
-            for g in range(4)
-        ]
+        rows = []
+        for p in range(4):
+            for g in range(4):
+                place = (chip(p, g, kh), slice(kh * 32, kh * 32 + 32))
+                own, sib = own_ref[place].astype(F32), sib_ref[place].astype(F32)
+                rows.append(jnp.where(flip() == (g >> 1), own, sib))
         turned = jnp.concatenate(rows, axis=0).T
         big = jnp.concatenate([jnp.where(lane_k == k, turned, 0.0) for k in range(4)], axis=0)
-        copies[kh].wait()
-        mixed.append(dot(x_ref[kh], big.astype(BF)).astype(BF))
+        mixed.append(dot(x_ref[:, kh * 512 : (kh + 1) * 512], big.astype(BF)).astype(BF))
     even = ((iota((mixed[0].shape[0], 128), 1) >> 5) & 1) == 0
     for p in range(4):
         lanes = slice(p * 128, (p + 1) * 128)
@@ -150,7 +176,7 @@
         out_ref[2 * p + 1] = jnp.where(even, b, a)
 
 
-def mix(x, gathered):
+def mix(x, own, sibling):
     rows = x.shape[0]
     return pl.pallas_call(
         mix_kernel,
@@ -158,12 +184,10 @@
             jax.ShapeDtypeStruct((8, rows, 128), BF),
             jax.ShapeDtypeStruct((2, 512, 512), BF),
         ),
-        in_specs=[pl.BlockSpec(memory_space=pltpu.HBM), pl.BlockSpec()],
-        scratch_shapes=[pltpu.VMEM((2, rows, 512), BF), pltpu.SemaphoreType.DMA((2,))],
         compiler_params=params(),
         cost_estimate=cost(rows * 1024 * 1024, 4 * rows * 1024),
         name="mix",
-    )(in_hbm(x), gathered)
+    )(x, own, sibling)
 
 
 def middle_kernel(in_ref, back_ref, target_ref, student_ref, left_ref, out_ref):
@@ -190,7 +214,7 @@
         a, b = outs[0][:, lanes], outs[1][:, lanes]
         out_ref[2 * p] = jnp.where(low, a, b)
         out_ref[2 * p + 1] = jnp.where(low, b, a)
-    ordered = exchange(total, 8, 16).astype(BF)
+    ordered = exchange(total, 8, 16)
     for s in range(16):
         left_ref[s] = ordered[s * 32 : (s + 1) * 32, :]
 
@@ -201,7 +225,7 @@
         middle_kernel,
         out_shape=(
             pltpu.VMEM((rows, 1024), BF),
-            jax.ShapeDtypeStruct((16, 32, 128), BF),
+            jax.ShapeDtypeStruct((16, 32, 128), F32),
             jax.ShapeDtypeStruct((8, rows, 128), BF),
         ),
         compiler_params=params(),
@@ -210,10 +234,10 @@
     )(received, back, target)
 
 
-def grads_kernel(student_ref, left_ref, back_ref, x_ref, student_hbm, out_ref, sem):
+def grads_kernel(student_ref, left_ref, back_ref, x_ref, student_hbm, mine_ref, other_ref, sem):
     copy = pltpu.make_async_copy(student_ref, student_hbm, sem)
     copy.start()
-    par = parity()
+    same = flip() == 0
     returned = split([back_ref[j] for j in range(8)])
     row_k = (iota((512, 128), 0) >> 3) & 3
     for kh in range(2):
@@ -221,13 +245,16 @@
         kept = jnp.zeros((512, 128), F32)
         for k in range(4):
             kept = jnp.where(row_k == k, full[:, k * 128 : (k + 1) * 128], kept)
-        kept = kept.astype(BF)
         for p in range(4):
-            for g in range(4):
+            for g in range(2):
                 n = (p * 4 + g) * 32
-                out_ref[source(p, g, kh, par), kh * 32 : kh * 32 + 32, :] = kept[n : n + 32, :]
-    for s in range(16):
-        out_ref[s, 64:96, :] = left_ref[s]
+                a, b = kept[n : n + 32], kept[n + 64 : n + 96]
+                place = (chip(p, g, kh), slice(kh * 32, kh * 32 + 32))
+                mine_ref[place] = jnp.where(same, a, b)
+                other_ref[place] = jnp.where(same, b, a).astype(BF)
+    for n in range(8):
+        mine_ref[n, 64:96, :] = left_ref[2 * n + core()]
+        other_ref[n, 64:96, :] = left_ref[2 * n + 1 - core()].astype(BF)
     copy.wait()
 
 
@@ -237,9 +264,10 @@
         grads_kernel,
         out_shape=(
             pltpu.HBM(student.shape, BF),
-            jax.ShapeDtypeStruct((16, 96, 128), BF),
+            jax.ShapeDtypeStruct((8, 96, 128), F32),
+            jax.ShapeDtypeStruct((8, 96, 128), BF),
         ),
-        out_specs=(pl.BlockSpec(memory_space=pltpu.HBM), pl.BlockSpec()),
+        out_specs=(pl.BlockSpec(memory_space=pltpu.HBM), pl.BlockSpec(), pl.BlockSpec()),
         scratch_shapes=[pltpu.SemaphoreType.DMA],
         compiler_params=params(),
         cost_estimate=cost(2 * rows * 1024 * 1024, 8 * rows * 1024),
@@ -249,7 +277,7 @@
 
 def sum_kernel(scale, in_ref, right_ref, left_ref):
     total = in_ref[0].astype(F32)
-    for s in range(1, 16):
+    for s in range(1, 8):
         total = total + in_ref[s].astype(F32)
     total = total * scale
     right_ref[...] = total[:64].reshape(8, 8, 128)
@@ -273,13 +301,18 @@
 def shards(tokens, right_factor, left_factor, target):
     rows = tokens.shape[0]
     scale = 1.0 / math.sqrt(rows * lax.axis_size("seq"))
-    gathered = lax.all_to_all(pack(right_factor, left_factor), "seq", 0, 0, tiled=True)
-    mixed, back = mix(tokens, gathered)
+    chips = [[2 * n + c for n in range(8)] for c in range(2)]
+    across = [(n, n ^ 1) for n in range(16)]
+    own = lax.all_to_all(
+        pack(right_factor, left_factor), "seq", 0, 0, tiled=True, axis_index_groups=chips
+    )
+    mixed, back = mix(fetch(tokens, own), own, lax.ppermute(own, "seq", across))
     received = lax.all_to_all(mixed, "blk", 0, 0, tiled=True)
     student, left, out = middle(received, back, target)
     returned = lax.all_to_all(out, "blk", 0, 0, tiled=True)
-    student, terms = grads(student, left, returned, tokens)
-    terms = lax.all_to_all(terms, "seq", 0, 0, tiled=True)
+    student, mine, other = grads(student, left, returned, tokens)
+    terms = (mine + lax.ppermute(other, "seq", across).astype(F32)).astype(BF)
+    terms = lax.all_to_all(terms, "seq", 0, 0, tiled=True, axis_index_groups=chips)
     right_grad, left_grad = sums(terms, scale)
     return (student, right_grad, left_grad)
 

time: 106 us -> 104 us (0.981)
  blocking collectives: 94 us -> 89.5 us
  waiting for transfers between devices: 0 us -> 1.43 us
    all_to_all x2, blocking collectives: 35 us -> 27.9 us  [the longest x1 16.3 us: shards(): lax.all_to_all(pack(right_factor, left_factor), 'seq', 0, 0, tiled=True,...]
    pallas_call x0 -> x1, Pallas kernels: none -> 1.6 us  [fetch(): pl.pallas_call(fetch_kernel, in_specs=[pl.BlockSpec(memory_space=pltpu.HB...]
    ppermute x0 -> x2, waiting for transfers between devices: none -> 1.43 us  [the longest x1 1.43 us: shards(): terms = (mine + lax.ppermute(other, 'seq', across).astype(F32)).astype(BF)]
    all_to_all x1, blocking collectives: 28.3 us -> 29.7 us  [shards(): returned = lax.all_to_all(out, 'blk', 0, 0, tiled=True)]
    all_to_all x1, blocking collectives: 30.8 us -> 31.9 us  [shards(): received = lax.all_to_all(mixed, 'blk', 0, 0, tiled=True)]
    pallas_call x1, Pallas kernels: 2.7 us -> 1.61 us  [mix(): pl.pallas_call(mix_kernel, out_shape=(jax.ShapeDtypeStruct((8, rows, 128)...]
  transfers between devices with their start and end apart: 0 -> 2, of which waited for: 0 -> 1; matrix products, arithmetic and copies ran while one was open for 0% -> 0% of each run, Pallas kernels for 0% -> 2%
where the time goes in v4:
time: 104 us; the launch traced here: 103 us
  blocking collectives  89.5 us (86%)
  Pallas kernels  11.5 us (11%)
  waiting for transfers between devices  1.43 us (1%)
    all_to_all x1, blocking collectives, shards(): received = lax.all_to_all(mixed, 'blk', 0, 0, tiled=True)  31.9 us
    all_to_all x1, blocking collectives, shards(): returned = lax.all_to_all(out, 'blk', 0, 0, tiled=True)  29.7 us
    all_to_all x1, blocking collectives, shards(): lax.all_to_all(pack(right_factor, left_factor), 'seq', 0, 0, tiled=True,...  16.3 us
    all_to_all x1, blocking collectives, shards(): lax.all_to_all(terms, 'seq', 0, 0, tiled=True, axis_index_groups=chips)  11.6 us
    pallas_call x1, Pallas kernels, middle(): pl.pallas_call(middle_kernel, out_shape=(pltpu.VMEM((rows, 1024), BF), ja...  5.4 us
  transfers between devices with their start and end apart: 2, of which 1 were waited for; matrix products, arithmetic and copies ran while one was open for 0% of the time, Pallas kernels for 2%

profile of v4, /device:TPU:0, one launch (start us, length us, event | category | flops | bytes accessed | tf_op | source)
XLA Modules:
  0.0 103.3 jit_solution(11780799857642094502)
XLA Ops:
  0.6 0.8 pack.1
  1.5 16.3 %all_to_all.20.after_ref.own_ref = bf16[8,96,128]{2,1,0:T(8,128)(2,1)S(1)} all-to-all(bf16[8,96,128]{2,1,0:T(8,128)(2,1)S(1)} %pack.1), channel_id=1, replica_groups={{0,16,32,48,64,80,96,112},{8,24,40,56,72,88,104,120},{1,17,33,49,65,81,..., dimensions={0} | all-to-all | bytes 393216 | tf_op jit(solution)/shard_map/all_to_all | solution.py:306
  17.8 0.0 collective-permute-start
  17.8 1.6 %fetch.1.x_ref = bf16[1024,1024]{1,0:T(8,128)(2,1)S(1)} custom-call(bf16[1024,1024]{1,0:T(8,128)(2,1)} %x_ref.1, bf16[8,96,128]{2,1,0:T(8,128)(2,1)S(1)} %all_to_all.20.after_ref.own_ref), custom_call_target="tpu_custom_call" | custom-call | bytes 8388608 | tf_op jit(solution)/shard_map/fetch/pallas_call | solution.py:136
  19.4 0.0 collective-permute-done.sib_ref
  19.4 1.6 %mix.1 = (bf16[8,1024,128]{2,1,0:T(8,128)(2,1)S(1)}, bf16[2,512,512]{2,1,0:T(8,128)(2,1)S(1)}) custom-call(bf16[1024,1024]{1,0:T(8,128)(2,1)S(1)} %fetch.1.x_ref, bf16[8,96,128]{2,1,0:T(8,128)(2,1)S(1)} %all_to_all.20.after_ref.own_ref, bf16[8,96,128]{2,1,0:T(8,128)(2,1)S(1)} %collective-permute-done.sib_ref), custom_call_target="tpu_custom_call" | custom-call | flops 1073741824 | bytes 4194304 | tf_op jit(solution)/shard_map/mix/pallas_call | solution.py:181
  21.0 0.0 copy-start.1
  21.0 31.9 %all_to_all.21.in_ref = bf16[8,1024,128]{2,1,0:T(8,128)(2,1)S(1)} all-to-all(bf16[8,1024,128]{2,1,0:T(8,128)(2,1)S(1)} %get-tuple-element.13), channel_id=1, replica_groups=mesh['seq'=16,'blk'=8] {'blk'}, dimensions={0} | all-to-all | bytes 4194304 | tf_op jit(solution)/shard_map/all_to_all | solution.py:310
  53.0 0.0 copy-done.1
  53.0 5.4 %middle.1 = (bf16[1024,1024]{1,0:T(8,128)(2,1)S(1)}, f32[16,32,128]{2,1,0:T(8,128)S(1)}, bf16[8,1024,128]{2,1,0:T(8,128)(2,1)S(1)}) custom-call(bf16[8,1024,128]{2,1,0:T(8,128)(2,1)S(1)} %all_to_all.21.in_ref, bf16[2,512,512]{2,1,0:T(8,128)(2,1)S(1)} %get-tuple-element.14.back_ref, bf16[1024,1024]{1,0:T(8,128)(2,1)S(1)} %copy-done.1), custom_call_target="tpu_custom_call" | custom-call | flops 2147483648 | bytes 10485760 | tf_op jit(solution)/shard_map/middle/pallas_call | solution.py:224
  58.4 0.0 copy-start
  58.4 29.7 %all_to_all.22.back_ref = bf16[8,1024,128]{2,1,0:T(8,128)(2,1)S(1)} all-to-all(bf16[8,1024,128]{2,1,0:T(8,128)(2,1)S(1)} %get-tuple-element.17), channel_id=1, replica_groups=mesh['seq'=16,'blk'=8] {'blk'}, dimensions={0} | all-to-all | bytes 4194304 | tf_op jit(solution)/shard_map/all_to_all | solution.py:312
  88.0 0.0 copy-done
  88.0 1.4 %grads.1 = (bf16[1024,1024]{1,0:T(8,128)(2,1)}, f32[8,96,128]{2,1,0:T(8,128)S(1)}, bf16[8,96,128]{2,1,0:T(8,128)(2,1)S(1)}) custom-call(bf16[1024,1024]{1,0:T(8,128)(2,1)S(1)} %get-tuple-element.15.student_ref, f32[16,32,128]{2,1,0:T(8,128)S(1)} %get-tuple-element.16.left_ref, bf16[8,1024,128]{2,1,0:T(8,128)(2,1)S(1)} %all_to_all.22.back_ref, ...), custom_call_target="tpu_custom_call" | custom-call | flops 2147483648 | bytes 8388608 | tf_op jit(solution)/shard_map/grads/pallas_call | solution.py:263
  89.4 0.1 collective-permute-start.1
  89.5 1.4 %collective-permute-done.1 = bf16[8,96,128]{2,1,0:T(8,128)(2,1)S(1)} collective-permute-done((bf16[8,96,128]{2,1,0:T(8,128)(2,1)S(1)}, bf16[8,96,128]{2,1,0:T(8,128)(2,1)S(1)}, u32[]{:S(2)}, u32[]{:S(2)}) %collective-permute-start.1) | collective-permute-done | bytes 196640 | tf_op jit(solution)/shard_map/ppermute | solution.py:314
  91.0 11.6 %all_to_all.23.in_ref = bf16[8,96,128]{2,1,0:T(8,128)(2,1)S(1)} all-to-all(bf16[8,96,128]{2,1,0:T(8,128)(2,1)S(1)} %add_convert_fusion), channel_id=1, replica_groups={{0,16,32,48,64,80,96,112},{8,24,40,56,72,88,104,120},{1,17,33,49,65,81,..., dimensions={0} | all-to-all | bytes 393216 | tf_op jit(solution)/shard_map/all_to_all | solution.py:315
  102.6 0.7 sums.1
  (1 shorter events, 0.0 us)
Async XLA Ops:
  17.8 1.6 %collective-permute-start = (bf16[8,96,128]{2,1,0:T(8,128)(2,1)S(1)}, bf16[8,96,128]{2,1,0:T(8,128)(2,1)S(1)}, u32[]{:S(2)}, u32[]{:S(2)}) collective-permute-start(bf16[8,96,128]{2,1,0:T(8,128)(2,1)S(1)} %all_to_all.20.after_ref.own_ref), channel_id=1, source_target_pairs={{0,8},{8,0},{16,24},{24,16},{32,40},{40,32},{48,56},{56,48},{64,72... | collective-permute-start | bytes 589832 | tf_op jit(solution)/shard_map/ppermute | solution.py:309
  21.0 32.0 %copy-start.1 = (bf16[1024,1024]{1,0:T(8,128)(2,1)S(1)}, bf16[1024,1024]{1,0:T(8,128)(2,1)}, u32[]{:S(2)}) copy-start(bf16[1024,1024]{1,0:T(8,128)(2,1)} %target_ref.1) | copy-start | bytes 6291460
  58.4 29.7 %copy-start = (bf16[1024,1024]{1,0:T(8,128)(2,1)S(1)}, bf16[1024,1024]{1,0:T(8,128)(2,1)}, u32[]{:S(2)}) copy-start(bf16[1024,1024]{1,0:T(8,128)(2,1)} %x_ref.1) | copy-start | bytes 6291460
  89.4 1.5 %collective-permute-start.1 = (bf16[8,96,128]{2,1,0:T(8,128)(2,1)S(1)}, bf16[8,96,128]{2,1,0:T(8,128)(2,1)S(1)}, u32[]{:S(2)}, u32[]{:S(2)}) collective-permute-start(bf16[8,96,128]{2,1,0:T(8,128)(2,1)S(1)} %get-tuple-element.20), channel_id=1, source_target_pairs={{0,8},{8,0},{16,24},{24,16},{32,40},{40,32},{48,56},{56,48},{64,72... | collective-permute-start | bytes 589832 | tf_op jit(solution)/shard_map/ppermute | solution.py:314

commit v5 on v4

--- a/solution.py
+++ b/solution.py
@@ -81,15 +81,14 @@
     right = right_ref[...].astype(F32).reshape(64, 128)
     left = left_ref[...].astype(F32).reshape(64, 64)
     whole = jnp.concatenate([right, joined([left[:32], left[32:]])], axis=0).astype(BF)
-    for s in range(8):
-        out_ref[s] = whole
+    out_ref[...] = whole
 
 
 def pack(right, left):
     return pl.pallas_call(
         pack_kernel,
         in_specs=[pl.BlockSpec(memory_space=pltpu.HBM)] * 2,
-        out_shape=jax.ShapeDtypeStruct((8, 96, 128), BF),
+        out_shape=jax.ShapeDtypeStruct((96, 128), BF),
         scratch_shapes=[
             pltpu.VMEM(right.shape, BF),
             pltpu.VMEM(left.shape, BF),
@@ -100,6 +99,60 @@
     )(in_hbm(right), in_hbm(left))
 
 
+def pair_kernel(own_ref, sib_ref, after_ref, out_ref):
+    first = core() == 0
+    own, sib = own_ref[...].astype(F32), sib_ref[...].astype(F32)
+    low, high = jnp.where(first, own, sib).astype(BF), jnp.where(first, sib, own).astype(BF)
+    for n in range(8):
+        out_ref[n, 0:96, :] = low
+        out_ref[n, 96:192, :] = high
+
+
+def pair(own, sibling, after):
+    return pl.pallas_call(
+        pair_kernel,
+        in_specs=[pl.BlockSpec(), pl.BlockSpec(), pl.BlockSpec(memory_space=pl.ANY)],
+        out_shape=jax.ShapeDtypeStruct((8, 192, 128), BF),
+        compiler_params=params(8),
+        name="pair",
+    )(own, sibling, after)
+
+
+def plane():
+    return lax.rem(lax.div(lax.axis_index("seq"), 2), 2)
+
+
+def other_kernel(g_ref, out_ref):
+    there = 1 - plane()
+    for z in range(4):
+        out_ref[z] = g_ref[2 * z + there]
+
+
+def other_half(gathered):
+    return pl.pallas_call(
+        other_kernel,
+        out_shape=jax.ShapeDtypeStruct((4, 192, 128), BF),
+        compiler_params=params(8),
+        name="other_half",
+    )(gathered)
+
+
+def pass_kernel(x_ref, turn_ref, out_ref):
+    pass
+
+
+def pass_on(x, turn):
+    return pl.pallas_call(
+        pass_kernel,
+        out_shape=jax.ShapeDtypeStruct(x.shape, x.dtype),
+        in_specs=[pl.BlockSpec(memory_space=pl.ANY)] * 2,
+        out_specs=pl.BlockSpec(memory_space=pl.ANY),
+        input_output_aliases={0: 0},
+        compiler_params=params(8),
+        name="pass_on",
+    )(x, turn)
+
+
 def exchange(x, a, b):
     low = iota((8, x.shape[1]), 0) < 4
 
@@ -144,14 +197,23 @@
     )(in_hbm(x), after)
 
 
-def mix_kernel(x_ref, own_ref, sib_ref, out_ref, back_ref):
+def mix_kernel(x_ref, all_ref, near_ref, far_ref, out_ref, back_ref, g_ref):
+    @pl.when(core() == 0)
+    def _():
+        g_ref[...] = all_ref[...]
+
+    @pl.when(core() == 1)
+    def _():
+        here = plane()
+        for z in range(4):
+            g_ref[2 * z + here] = near_ref[z]
+            g_ref[2 * z + 1 - here] = far_ref[z]
+
     par = parity()
-    first = core() == 0
-    rows = []
-    for n in range(8):
-        own, sib = own_ref[n, 64:96, :].astype(F32), sib_ref[n, 64:96, :].astype(F32)
-        rows += [jnp.where(first, own, sib), jnp.where(first, sib, own)]
-    packed = jnp.concatenate(rows, axis=0)
+    packed = jnp.concatenate(
+        [g_ref[n, c * 96 + 64 : c * 96 + 96, :].astype(F32) for n in range(8) for c in range(2)],
+        axis=0,
+    )
     ordered = exchange(packed, 16, 8).astype(BF)
     for h in range(2):
         full = dot(ordered, spread(h, par))
@@ -162,9 +224,9 @@
         rows = []
         for p in range(4):
             for g in range(4):
-                place = (chip(p, g, kh), slice(kh * 32, kh * 32 + 32))
-                own, sib = own_ref[place].astype(F32), sib_ref[place].astype(F32)
-                rows.append(jnp.where(flip() == (g >> 1), own, sib))
+                n, k = chip(p, g, kh), kh * 32
+                low, high = g_ref[n, k : k + 32, :], g_ref[n, k + 96 : k + 128, :]
+                rows.append(jnp.where(par == (g >> 1), low.astype(F32), high.astype(F32)))
         turned = jnp.concatenate(rows, axis=0).T
         big = jnp.concatenate([jnp.where(lane_k == k, turned, 0.0) for k in range(4)], axis=0)
         mixed.append(dot(x_ref[:, kh * 512 : (kh + 1) * 512], big.astype(BF)).astype(BF))
@@ -176,7 +238,7 @@
         out_ref[2 * p + 1] = jnp.where(even, b, a)
 
 
-def mix(x, own, sibling):
+def mix(x, gathered, near, far):
     rows = x.shape[0]
     return pl.pallas_call(
         mix_kernel,
@@ -184,10 +246,11 @@
             jax.ShapeDtypeStruct((8, rows, 128), BF),
             jax.ShapeDtypeStruct((2, 512, 512), BF),
         ),
+        scratch_shapes=[pltpu.VMEM((8, 192, 128), BF)],
         compiler_params=params(),
         cost_estimate=cost(rows * 1024 * 1024, 4 * rows * 1024),
         name="mix",
-    )(x, own, sibling)
+    )(x, gathered, near, far)
 
 
 def middle_kernel(in_ref, back_ref, target_ref, student_ref, left_ref, out_ref):
@@ -303,14 +366,26 @@
     scale = 1.0 / math.sqrt(rows * lax.axis_size("seq"))
     chips = [[2 * n + c for n in range(8)] for c in range(2)]
     across = [(n, n ^ 1) for n in range(16)]
-    own = lax.all_to_all(
-        pack(right_factor, left_factor), "seq", 0, 0, tiled=True, axis_index_groups=chips
-    )
-    mixed, back = mix(fetch(tokens, own), own, lax.ppermute(own, "seq", across))
+    own = pack(right_factor, left_factor)
+    x = fetch(tokens, own)
+    share = pair(own, lax.ppermute(own, "seq", across), x)
+
+    def gather(share):
+        return lax.all_to_all(share, "seq", 0, 0, tiled=True, axis_index_groups=chips)
+
+    def gather_z(share):
+        lines = [[4 * z + n for z in range(4)] for n in range(4)]
+        return lax.all_to_all(share, "seq", 0, 0, tiled=True, axis_index_groups=lines)
+
+    first = lax.axis_index("seq") % 2 == 0
+    gathered = lax.cond(first, gather, lambda share: share, share)
+    far = lax.ppermute(other_half(gathered), "seq", [(2 * n, 2 * n + 1) for n in range(8)])
+    near = lax.cond(first, lambda share: share, gather_z, pass_on(share[:4], far))
+    mixed, back = mix(x, gathered, near, far)
     received = lax.all_to_all(mixed, "blk", 0, 0, tiled=True)
     student, left, out = middle(received, back, target)
     returned = lax.all_to_all(out, "blk", 0, 0, tiled=True)
-    student, mine, other = grads(student, left, returned, tokens)
+    student, mine, other = grads(student, left, returned, x)
     terms = (mine + lax.ppermute(other, "seq", across).astype(F32)).astype(BF)
     terms = lax.all_to_all(terms, "seq", 0, 0, tiled=True, axis_index_groups=chips)
     right_grad, left_grad = sums(terms, scale)

time: 104 us -> 102 us (0.981)
  blocking collectives: 89.5 us -> 80.7 us
  starting transfers between devices: 0.09 us -> 6.63 us
    all_to_all x1, blocking collectives: 31.9 us -> 26.1 us  [shards(): received = lax.all_to_all(mixed, 'blk', 0, 0, tiled=True)]
    ppermute x1, starting transfers between devices: 0.09 us -> 5.24 us  [shards(): terms = (mine + lax.ppermute(other, 'seq', across).astype(F32)).astype(BF)]
    all_to_all x1, blocking collectives: 29.7 us -> 25.5 us  [shards(): returned = lax.all_to_all(out, 'blk', 0, 0, tiled=True)]
    ppermute x1 -> x2, starting transfers between devices: 0.01 us -> 1.39 us  [the longest x1 1.3 us: shards(): lax.ppermute(other_half(gathered), 'seq', [(2 * n, 2 * n + 1) for n in ra...]
    all_to_all x1, blocking collectives: 16.3 us -> 17.4 us  [gather(): lax.all_to_all(share, 'seq', 0, 0, tiled=True, axis_index_groups=chips)]
  transfers between devices with their start and end apart: 2 -> 3, of which waited for: 1 -> 2; matrix products, arithmetic and copies ran while one was open for 0% -> 0% of each run, Pallas kernels for 2% -> 2%
where the time goes in v5:
time: 102 us
  blocking collectives  80.7 us (79%)
  Pallas kernels  11.6 us (11%)
  starting transfers between devices  6.63 us (6%)
  waiting for transfers between devices  2.09 us (2%)
    all_to_all x1, blocking collectives, shards(): received = lax.all_to_all(mixed, 'blk', 0, 0, tiled=True)  26.1 us
    all_to_all x1, blocking collectives, shards(): returned = lax.all_to_all(out, 'blk', 0, 0, tiled=True)  25.5 us
    all_to_all x1, blocking collectives, gather(): lax.all_to_all(share, 'seq', 0, 0, tiled=True, axis_index_groups=chips)  17.4 us
    all_to_all x1, blocking collectives, shards(): lax.all_to_all(terms, 'seq', 0, 0, tiled=True, axis_index_groups=chips)  11.7 us
    pallas_call x1, Pallas kernels, middle(): pl.pallas_call(middle_kernel, out_shape=(pltpu.VMEM((rows, 1024), BF), ja...  5.4 us
    ppermute x1, starting transfers between devices, shards(): terms = (mine + lax.ppermute(other, 'seq', across).astype(F32)).astype(BF)  5.24 us
  transfers between devices with their start and end apart: 3, of which 2 were waited for; matrix products, arithmetic and copies ran while one was open for 0% of the time, Pallas kernels for 2%

profile of v5, /device:TPU:0, one launch (start us, length us, event | category | flops | bytes accessed | tf_op | source)
XLA Modules:
  0.0 101.8 jit_solution(17255179400580888654)
XLA Ops:
  0.6 0.8 pack.1.after_ref.own_ref
  1.5 0.1 collective-permute-start
  1.6 1.6 %fetch.1.after_ref.x_ref = bf16[1024,1024]{1,0:T(8,128)(2,1)S(1)} custom-call(bf16[1024,1024]{1,0:T(8,128)(2,1)} %x_hbm.1, bf16[96,128]{1,0:T(8,128)(2,1)S(1)} %pack.1.after_ref.own_ref), custom_call_target="tpu_custom_call" | custom-call | bytes 8388608 | tf_op jit(solution)/shard_map/fetch/pallas_call | solution.py:189
  3.2 0.0 collective-permute-done.sib_ref
  3.2 17.5 %conditional.2 = (bf16[8,192,128]{2,1,0:T(8,128)(2,1)S(1)}) conditional(s32[]{:T(128)} %convert_element_type.10, bf16[8,192,128]{2,1,0:T(8,128)(2,1)S(1)} %pair.1, bf16[8,192,128]{2,1,0:T(8,128)(2,1)S(1)} %pair.1), branch_computations={%region_0.1_spmd, %region_1.2_spmd} | conditional | bytes 786440 | solution.py:381
  3.3 17.4 %all_to_all.23 = bf16[8,192,128]{2,1,0:T(8,128)(2,1)S(1)} all-to-all(bf16[8,192,128]{2,1,0:T(8,128)(2,1)S(1)} %param.1), channel_id=1, replica_groups={{0,16,32,48,64,80,96,112},{8,24,40,56,72,88,104,120},{1,17,33,49,65,81,..., dimensions={0} | all-to-all | bytes 786432 | tf_op jit(solution)/shard_map/cond/branch_1_fun/all_to_all | solution.py:374
  20.7 1.3 %collective-permute-start.1 = (bf16[4,192,128]{2,1,0:T(8,128)(2,1)S(1)}, bf16[4,192,128]{2,1,0:T(8,128)(2,1)S(1)}, u32[]{:S(2)}, u32[]{:S(2)}) collective-permute-start(bf16[4,192,128]{2,1,0:T(8,128)(2,1)S(1)} %other_half.1), channel_id=1, source_target_pairs={{0,8},{16,24},{32,40},{48,56},{64,72},{80,88},{96,104},{112,120},{... | collective-permute-start | bytes 589832 | tf_op jit(solution)/shard_map/ppermute | solution.py:382
  22.1 1.0 %collective-permute-done.1.turn_ref.far_ref = bf16[4,192,128]{2,1,0:T(8,128)(2,1)S(1)} collective-permute-done((bf16[4,192,128]{2,1,0:T(8,128)(2,1)S(1)}, bf16[4,192,128]{2,1,0:T(8,128)(2,1)S(1)}, u32[]{:S(2)}, u32[]{:S(2)}) %collective-permute-start.1) | collective-permute-done | bytes 196640 | tf_op jit(solution)/shard_map/ppermute | solution.py:382
  23.1 1.6 %mix.1 = (bf16[8,1024,128]{2,1,0:T(8,128)(2,1)S(1)}, bf16[2,512,512]{2,1,0:T(8,128)(2,1)S(1)}) custom-call(bf16[1024,1024]{1,0:T(8,128)(2,1)S(1)} %fetch.1.after_ref.x_ref, bf16[8,192,128]{2,1,0:T(8,128)(2,1)S(1)} %get-tuple-element.33.g_ref.all_ref, bf16[4,192,128]{2,1,0:T(8,128)(2,1)S(1)} %get-tuple-element.34.near_ref, ...), custom_call_target="tpu_custom_call" | custom-call | flops 1073741824 | bytes 4194304 | tf_op jit(solution)/shard_map/mix/pallas_call | solution.py:243
  24.7 0.0 copy-start
  24.7 26.1 %all_to_all.25.in_ref = bf16[8,1024,128]{2,1,0:T(8,128)(2,1)S(1)} all-to-all(bf16[8,1024,128]{2,1,0:T(8,128)(2,1)S(1)} %get-tuple-element.23), channel_id=1, replica_groups=mesh['seq'=16,'blk'=8] {'blk'}, dimensions={0} | all-to-all | bytes 4194304 | tf_op jit(solution)/shard_map/all_to_all | solution.py:385
  50.8 0.0 copy-done
  50.8 5.4 %middle.1 = (bf16[1024,1024]{1,0:T(8,128)(2,1)S(1)}, f32[16,32,128]{2,1,0:T(8,128)S(1)}, bf16[8,1024,128]{2,1,0:T(8,128)(2,1)S(1)}) custom-call(bf16[8,1024,128]{2,1,0:T(8,128)(2,1)S(1)} %all_to_all.25.in_ref, bf16[2,512,512]{2,1,0:T(8,128)(2,1)S(1)} %get-tuple-element.24.back_ref, bf16[1024,1024]{1,0:T(8,128)(2,1)S(1)} %copy-done), custom_call_target="tpu_custom_call" | custom-call | flops 2147483648 | bytes 10485760 | tf_op jit(solution)/shard_map/middle/pallas_call | solution.py:287
  56.3 25.5 %all_to_all.26.back_ref = bf16[8,1024,128]{2,1,0:T(8,128)(2,1)S(1)} all-to-all(bf16[8,1024,128]{2,1,0:T(8,128)(2,1)S(1)} %get-tuple-element.27), channel_id=1, replica_groups=mesh['seq'=16,'blk'=8] {'blk'}, dimensions={0} | all-to-all | bytes 4194304 | tf_op jit(solution)/shard_map/all_to_all | solution.py:387
  81.7 1.4 %grads.1 = (bf16[1024,1024]{1,0:T(8,128)(2,1)}, f32[8,96,128]{2,1,0:T(8,128)S(1)}, bf16[8,96,128]{2,1,0:T(8,128)(2,1)S(1)}) custom-call(bf16[1024,1024]{1,0:T(8,128)(2,1)S(1)} %get-tuple-element.25.student_ref, f32[16,32,128]{2,1,0:T(8,128)S(1)} %get-tuple-element.26.left_ref, bf16[8,1024,128]{2,1,0:T(8,128)(2,1)S(1)} %all_to_all.26.back_ref, ...), custom_call_target="tpu_custom_call" | custom-call | flops 2147483648 | bytes 8388608 | tf_op jit(solution)/shard_map/grads/pallas_call | solution.py:326
  83.1 5.2 %collective-permute-start.2 = (bf16[8,96,128]{2,1,0:T(8,128)(2,1)S(1)}, bf16[8,96,128]{2,1,0:T(8,128)(2,1)S(1)}, u32[]{:S(2)}, u32[]{:S(2)}) collective-permute-start(bf16[8,96,128]{2,1,0:T(8,128)(2,1)S(1)} %get-tuple-element.30), channel_id=1, source_target_pairs={{0,8},{8,0},{16,24},{24,16},{32,40},{40,32},{48,56},{56,48},{64,72... | collective-permute-start | bytes 589832 | tf_op jit(solution)/shard_map/ppermute | solution.py:389
  88.3 1.1 %collective-permute-done.2 = bf16[8,96,128]{2,1,0:T(8,128)(2,1)S(1)} collective-permute-done((bf16[8,96,128]{2,1,0:T(8,128)(2,1)S(1)}, bf16[8,96,128]{2,1,0:T(8,128)(2,1)S(1)}, u32[]{:S(2)}, u32[]{:S(2)}) %collective-permute-start.2) | collective-permute-done | bytes 196640 | tf_op jit(solution)/shard_map/ppermute | solution.py:389
  89.4 11.7 %all_to_all.27.in_ref = bf16[8,96,128]{2,1,0:T(8,128)(2,1)S(1)} all-to-all(bf16[8,96,128]{2,1,0:T(8,128)(2,1)S(1)} %add_convert_fusion), channel_id=1, replica_groups={{0,16,32,48,64,80,96,112},{8,24,40,56,72,88,104,120},{1,17,33,49,65,81,..., dimensions={0} | all-to-all | bytes 393216 | tf_op jit(solution)/shard_map/all_to_all | solution.py:390
  101.1 0.7 sums.1
  (6 shorter events, 0.1 us)
Async XLA Ops:
  1.5 1.7 %collective-permute-start = (bf16[96,128]{1,0:T(8,128)(2,1)S(1)}, bf16[96,128]{1,0:T(8,128)(2,1)S(1)}, u32[]{:S(2)}, u32[]{:S(2)}) collective-permute-start(bf16[96,128]{1,0:T(8,128)(2,1)S(1)} %pack.1.after_ref.own_ref), channel_id=1, source_target_pairs={{0,8},{8,0},{16,24},{24,16},{32,40},{40,32},{48,56},{56,48},{64,72... | collective-permute-start | bytes 73736 | tf_op jit(solution)/shard_map/ppermute | solution.py:371
  20.7 2.4 %collective-permute-start.1 = (bf16[4,192,128]{2,1,0:T(8,128)(2,1)S(1)}, bf16[4,192,128]{2,1,0:T(8,128)(2,1)S(1)}, u32[]{:S(2)}, u32[]{:S(2)}) collective-permute-start(bf16[4,192,128]{2,1,0:T(8,128)(2,1)S(1)} %other_half.1), channel_id=1, source_target_pairs={{0,8},{16,24},{32,40},{48,56},{64,72},{80,88},{96,104},{112,120},{... | collective-permute-start | bytes 589832 | tf_op jit(solution)/shard_map/ppermute | solution.py:382
  24.7 26.2 %copy-start = (bf16[1024,1024]{1,0:T(8,128)(2,1)S(1)}, bf16[1024,1024]{1,0:T(8,128)(2,1)}, u32[]{:S(2)}) copy-start(bf16[1024,1024]{1,0:T(8,128)(2,1)} %target_ref.1) | copy-start | bytes 6291460
  83.1 6.3 %collective-permute-start.2 = (bf16[8,96,128]{2,1,0:T(8,128)(2,1)S(1)}, bf16[8,96,128]{2,1,0:T(8,128)(2,1)S(1)}, u32[]{:S(2)}, u32[]{:S(2)}) collective-permute-start(bf16[8,96,128]{2,1,0:T(8,128)(2,1)S(1)} %get-tuple-element.30), channel_id=1, source_target_pairs={{0,8},{8,0},{16,24},{24,16},{32,40},{40,32},{48,56},{56,48},{64,72... | collective-permute-start | bytes 589832 | tf_op jit(solution)/shard_map/ppermute | solution.py:389

commit v6 on v5

--- a/solution.py
+++ b/solution.py
@@ -180,9 +180,11 @@
 
 
 def fetch_kernel(x_hbm, after_ref, out_ref, sem):
-    copy = pltpu.make_async_copy(x_hbm, out_ref, sem)
-    copy.start()
-    copy.wait()
+    @pl.when(core() == 0)
+    def _():
+        copy = pltpu.make_async_copy(x_hbm, out_ref, sem)
+        copy.start()
+        copy.wait()
 
 
 def fetch(x, after):
@@ -197,18 +199,7 @@
     )(in_hbm(x), after)
 
 
-def mix_kernel(x_ref, all_ref, near_ref, far_ref, out_ref, back_ref, g_ref):
-    @pl.when(core() == 0)
-    def _():
-        g_ref[...] = all_ref[...]
-
-    @pl.when(core() == 1)
-    def _():
-        here = plane()
-        for z in range(4):
-            g_ref[2 * z + here] = near_ref[z]
-            g_ref[2 * z + 1 - here] = far_ref[z]
-
+def mix_body(x_ref, g_ref, out_ref, back_ref):
     par = parity()
     packed = jnp.concatenate(
         [g_ref[n, c * 96 + 64 : c * 96 + 96, :].astype(F32) for n in range(8) for c in range(2)],
@@ -238,7 +229,24 @@
         out_ref[2 * p + 1] = jnp.where(even, b, a)
 
 
-def mix(x, gathered, near, far):
+def mix_kernel(x_hbm, x_ref, all_ref, near_ref, far_ref, out_ref, back_ref, g_ref, late_ref, sem):
+    @pl.when(core() == 0)
+    def _():
+        mix_body(x_ref, all_ref, out_ref, back_ref)
+
+    @pl.when(core() == 1)
+    def _():
+        copy = pltpu.make_async_copy(x_hbm, late_ref, sem)
+        copy.start()
+        here = plane()
+        for z in range(4):
+            g_ref[2 * z + here] = near_ref[z]
+            g_ref[2 * z + 1 - here] = far_ref[z]
+        copy.wait()
+        mix_body(late_ref, g_ref, out_ref, back_ref)
+
+
+def mix(tokens, x, gathered, near, far):
     rows = x.shape[0]
     return pl.pallas_call(
         mix_kernel,
@@ -246,11 +254,16 @@
             jax.ShapeDtypeStruct((8, rows, 128), BF),
             jax.ShapeDtypeStruct((2, 512, 512), BF),
         ),
-        scratch_shapes=[pltpu.VMEM((8, 192, 128), BF)],
+        in_specs=[pl.BlockSpec(memory_space=pltpu.HBM)] + [pl.BlockSpec()] * 4,
+        scratch_shapes=[
+            pltpu.VMEM((8, 192, 128), BF),
+            pltpu.VMEM(x.shape, BF),
+            pltpu.SemaphoreType.DMA,
+        ],
         compiler_params=params(),
         cost_estimate=cost(rows * 1024 * 1024, 4 * rows * 1024),
         name="mix",
-    )(x, gathered, near, far)
+    )(in_hbm(tokens), x, gathered, near, far)
 
 
 def middle_kernel(in_ref, back_ref, target_ref, student_ref, left_ref, out_ref):
@@ -381,11 +394,11 @@
     gathered = lax.cond(first, gather, lambda share: share, share)
     far = lax.ppermute(other_half(gathered), "seq", [(2 * n, 2 * n + 1) for n in range(8)])
     near = lax.cond(first, lambda share: share, gather_z, pass_on(share[:4], far))
-    mixed, back = mix(x, gathered, near, far)
+    mixed, back = mix(tokens, x, gathered, near, far)
     received = lax.all_to_all(mixed, "blk", 0, 0, tiled=True)
     student, left, out = middle(received, back, target)
     returned = lax.all_to_all(out, "blk", 0, 0, tiled=True)
-    student, mine, other = grads(student, left, returned, x)
+    student, mine, other = grads(student, left, returned, tokens)
     terms = (mine + lax.ppermute(other, "seq", across).astype(F32)).astype(BF)
     terms = lax.all_to_all(terms, "seq", 0, 0, tiled=True, axis_index_groups=chips)
     right_grad, left_grad = sums(terms, scale)

time: 102 us -> 101 us (level)
  blocking collectives: 80.7 us -> 77.9 us
  starting transfers between devices: 6.63 us -> 8.01 us
    all_to_all x1, blocking collectives: 26.1 us -> 24.6 us  [shards(): received = lax.all_to_all(mixed, 'blk', 0, 0, tiled=True)]
    ppermute x1, starting transfers between devices: 5.24 us -> 6.63 us  [shards(): terms = (mine + lax.ppermute(other, 'seq', across).astype(F32)).astype(BF)]
    all_to_all x1, blocking collectives: 25.5 us -> 24.2 us  [shards(): returned = lax.all_to_all(out, 'blk', 0, 0, tiled=True)]
where the time goes in v6:
time: 101 us; the launch traced here: 100 us
  blocking collectives  77.9 us (77%)
  Pallas kernels  11.6 us (11%)
  starting transfers between devices  8.01 us (8%)
  waiting for transfers between devices  2.09 us (2%)
    all_to_all x1, blocking collectives, shards(): received = lax.all_to_all(mixed, 'blk', 0, 0, tiled=True)  24.6 us
    all_to_all x1, blocking collectives, shards(): returned = lax.all_to_all(out, 'blk', 0, 0, tiled=True)  24.2 us
    all_to_all x1, blocking collectives, gather(): lax.all_to_all(share, 'seq', 0, 0, tiled=True, axis_index_groups=chips)  17.4 us
    all_to_all x1, blocking collectives, shards(): lax.all_to_all(terms, 'seq', 0, 0, tiled=True, axis_index_groups=chips)  11.7 us
    ppermute x1, starting transfers between devices, shards(): terms = (mine + lax.ppermute(other, 'seq', across).astype(F32)).astype(BF)  6.63 us
    pallas_call x1, Pallas kernels, middle(): pl.pallas_call(middle_kernel, out_shape=(pltpu.VMEM((rows, 1024), BF), ja...  5.4 us
  transfers between devices with their start and end apart: 3, of which 2 were waited for; matrix products, arithmetic and copies ran while one was open for 0% of the time, Pallas kernels for 2%

profile of v6, /device:TPU:0, one launch (start us, length us, event | category | flops | bytes accessed | tf_op | source)
XLA Modules:
  0.0 100.3 jit_solution(8504175678761957306)
XLA Ops:
  0.6 0.8 pack.1.after_ref.own_ref
  1.5 0.1 collective-permute-start
  1.6 1.6 %fetch.1.after_ref.x_ref = bf16[1024,1024]{1,0:T(8,128)(2,1)S(1)} custom-call(bf16[1024,1024]{1,0:T(8,128)(2,1)} %x_ref.1, bf16[96,128]{1,0:T(8,128)(2,1)S(1)} %pack.1.after_ref.own_ref), custom_call_target="tpu_custom_call" | custom-call | bytes 8388608 | tf_op jit(solution)/shard_map/fetch/pallas_call | solution.py:191
  3.2 0.0 collective-permute-done.sib_ref
  3.3 17.5 %conditional.2 = (bf16[8,192,128]{2,1,0:T(8,128)(2,1)S(1)}) conditional(s32[]{:T(128)} %convert_element_type.10, bf16[8,192,128]{2,1,0:T(8,128)(2,1)S(1)} %pair.1, bf16[8,192,128]{2,1,0:T(8,128)(2,1)S(1)} %pair.1), branch_computations={%region_0.1_spmd, %region_1.2_spmd} | conditional | bytes 786440 | solution.py:394
  3.3 17.4 %all_to_all.23 = bf16[8,192,128]{2,1,0:T(8,128)(2,1)S(1)} all-to-all(bf16[8,192,128]{2,1,0:T(8,128)(2,1)S(1)} %param.1), channel_id=1, replica_groups={{0,16,32,48,64,80,96,112},{8,24,40,56,72,88,104,120},{1,17,33,49,65,81,..., dimensions={0} | all-to-all | bytes 786432 | tf_op jit(solution)/shard_map/cond/branch_1_fun/all_to_all | solution.py:387
  20.7 1.3 %collective-permute-start.1 = (bf16[4,192,128]{2,1,0:T(8,128)(2,1)S(1)}, bf16[4,192,128]{2,1,0:T(8,128)(2,1)S(1)}, u32[]{:S(2)}, u32[]{:S(2)}) collective-permute-start(bf16[4,192,128]{2,1,0:T(8,128)(2,1)S(1)} %other_half.1), channel_id=1, source_target_pairs={{0,8},{16,24},{32,40},{48,56},{64,72},{80,88},{96,104},{112,120},{... | collective-permute-start | bytes 589832 | tf_op jit(solution)/shard_map/ppermute | solution.py:395
  22.1 1.0 %collective-permute-done.1.turn_ref.far_ref = bf16[4,192,128]{2,1,0:T(8,128)(2,1)S(1)} collective-permute-done((bf16[4,192,128]{2,1,0:T(8,128)(2,1)S(1)}, bf16[4,192,128]{2,1,0:T(8,128)(2,1)S(1)}, u32[]{:S(2)}, u32[]{:S(2)}) %collective-permute-start.1) | collective-permute-done | bytes 196640 | tf_op jit(solution)/shard_map/ppermute | solution.py:395
  23.1 1.6 %mix.1 = (bf16[8,1024,128]{2,1,0:T(8,128)(2,1)S(1)}, bf16[2,512,512]{2,1,0:T(8,128)(2,1)S(1)}) custom-call(bf16[1024,1024]{1,0:T(8,128)(2,1)} %x_ref.1, bf16[1024,1024]{1,0:T(8,128)(2,1)S(1)} %fetch.1.after_ref.x_ref, bf16[8,192,128]{2,1,0:T(8,128)(2,1)S(1)} %get-tuple-element.33.g_ref.all_ref, bf16[4,192,128]{2,1,0:T(8,128)(2,1)S(1)} %get-tuple-element.34.near_ref, ...), custom_call_target="tpu_custom_call" | custom-call | flops 1073741824 | bytes 4194304 | tf_op jit(solution)/shard_map/mix/pallas_call | solution.py:251
  24.7 0.0 copy-start.1
  24.7 24.6 %all_to_all.25.in_ref = bf16[8,1024,128]{2,1,0:T(8,128)(2,1)S(1)} all-to-all(bf16[8,1024,128]{2,1,0:T(8,128)(2,1)S(1)} %get-tuple-element.23), channel_id=1, replica_groups=mesh['seq'=16,'blk'=8] {'blk'}, dimensions={0} | all-to-all | bytes 4194304 | tf_op jit(solution)/shard_map/all_to_all | solution.py:398
  49.3 0.0 copy-done.1
  49.3 5.4 %middle.1 = (bf16[1024,1024]{1,0:T(8,128)(2,1)S(1)}, f32[16,32,128]{2,1,0:T(8,128)S(1)}, bf16[8,1024,128]{2,1,0:T(8,128)(2,1)S(1)}) custom-call(bf16[8,1024,128]{2,1,0:T(8,128)(2,1)S(1)} %all_to_all.25.in_ref, bf16[2,512,512]{2,1,0:T(8,128)(2,1)S(1)} %get-tuple-element.24.back_ref, bf16[1024,1024]{1,0:T(8,128)(2,1)S(1)} %copy-done.1), custom_call_target="tpu_custom_call" | custom-call | flops 2147483648 | bytes 10485760 | tf_op jit(solution)/shard_map/middle/pallas_call | solution.py:300
  54.7 0.0 copy-start
  54.7 24.2 %all_to_all.26.back_ref = bf16[8,1024,128]{2,1,0:T(8,128)(2,1)S(1)} all-to-all(bf16[8,1024,128]{2,1,0:T(8,128)(2,1)S(1)} %get-tuple-element.27), channel_id=1, replica_groups=mesh['seq'=16,'blk'=8] {'blk'}, dimensions={0} | all-to-all | bytes 4194304 | tf_op jit(solution)/shard_map/all_to_all | solution.py:400
  78.9 0.0 copy-done
  78.9 1.4 %grads.1 = (bf16[1024,1024]{1,0:T(8,128)(2,1)}, f32[8,96,128]{2,1,0:T(8,128)S(1)}, bf16[8,96,128]{2,1,0:T(8,128)(2,1)S(1)}) custom-call(bf16[1024,1024]{1,0:T(8,128)(2,1)S(1)} %get-tuple-element.25.student_ref, f32[16,32,128]{2,1,0:T(8,128)S(1)} %get-tuple-element.26.left_ref, bf16[8,1024,128]{2,1,0:T(8,128)(2,1)S(1)} %all_to_all.26.back_ref, ...), custom_call_target="tpu_custom_call" | custom-call | flops 2147483648 | bytes 8388608 | tf_op jit(solution)/shard_map/grads/pallas_call | solution.py:339
  80.2 6.6 %collective-permute-start.2 = (bf16[8,96,128]{2,1,0:T(8,128)(2,1)S(1)}, bf16[8,96,128]{2,1,0:T(8,128)(2,1)S(1)}, u32[]{:S(2)}, u32[]{:S(2)}) collective-permute-start(bf16[8,96,128]{2,1,0:T(8,128)(2,1)S(1)} %get-tuple-element.30), channel_id=1, source_target_pairs={{0,8},{8,0},{16,24},{24,16},{32,40},{40,32},{48,56},{56,48},{64,72... | collective-permute-start | bytes 589832 | tf_op jit(solution)/shard_map/ppermute | solution.py:402
  86.9 1.1 %collective-permute-done.2 = bf16[8,96,128]{2,1,0:T(8,128)(2,1)S(1)} collective-permute-done((bf16[8,96,128]{2,1,0:T(8,128)(2,1)S(1)}, bf16[8,96,128]{2,1,0:T(8,128)(2,1)S(1)}, u32[]{:S(2)}, u32[]{:S(2)}) %collective-permute-start.2) | collective-permute-done | bytes 196640 | tf_op jit(solution)/shard_map/ppermute | solution.py:402
  88.0 11.7 %all_to_all.27.in_ref = bf16[8,96,128]{2,1,0:T(8,128)(2,1)S(1)} all-to-all(bf16[8,96,128]{2,1,0:T(8,128)(2,1)S(1)} %add_convert_fusion), channel_id=1, replica_groups={{0,16,32,48,64,80,96,112},{8,24,40,56,72,88,104,120},{1,17,33,49,65,81,..., dimensions={0} | all-to-all | bytes 393216 | tf_op jit(solution)/shard_map/all_to_all | solution.py:403
  99.6 0.7 sums.1
  (6 shorter events, 0.1 us)
Async XLA Ops:
  1.5 1.7 %collective-permute-start = (bf16[96,128]{1,0:T(8,128)(2,1)S(1)}, bf16[96,128]{1,0:T(8,128)(2,1)S(1)}, u32[]{:S(2)}, u32[]{:S(2)}) collective-permute-start(bf16[96,128]{1,0:T(8,128)(2,1)S(1)} %pack.1.after_ref.own_ref), channel_id=1, source_target_pairs={{0,8},{8,0},{16,24},{24,16},{32,40},{40,32},{48,56},{56,48},{64,72... | collective-permute-start | bytes 73736 | tf_op jit(solution)/shard_map/ppermute | solution.py:384
  20.7 2.4 %collective-permute-start.1 = (bf16[4,192,128]{2,1,0:T(8,128)(2,1)S(1)}, bf16[4,192,128]{2,1,0:T(8,128)(2,1)S(1)}, u32[]{:S(2)}, u32[]{:S(2)}) collective-permute-start(bf16[4,192,128]{2,1,0:T(8,128)(2,1)S(1)} %other_half.1), channel_id=1, source_target_pairs={{0,8},{16,24},{32,40},{48,56},{64,72},{80,88},{96,104},{112,120},{... | collective-permute-start | bytes 589832 | tf_op jit(solution)/shard_map/ppermute | solution.py:395
  24.7 24.6 %copy-start.1 = (bf16[1024,1024]{1,0:T(8,128)(2,1)S(1)}, bf16[1024,1024]{1,0:T(8,128)(2,1)}, u32[]{:S(2)}) copy-start(bf16[1024,1024]{1,0:T(8,128)(2,1)} %target_ref.1) | copy-start | bytes 6291460
  54.7 24.2 %copy-start = (bf16[1024,1024]{1,0:T(8,128)(2,1)S(1)}, bf16[1024,1024]{1,0:T(8,128)(2,1)}, u32[]{:S(2)}) copy-start(bf16[1024,1024]{1,0:T(8,128)(2,1)} %x_ref.1) | copy-start | bytes 6291460
  80.2 7.7 %collective-permute-start.2 = (bf16[8,96,128]{2,1,0:T(8,128)(2,1)S(1)}, bf16[8,96,128]{2,1,0:T(8,128)(2,1)S(1)}, u32[]{:S(2)}, u32[]{:S(2)}) collective-permute-start(bf16[8,96,128]{2,1,0:T(8,128)(2,1)S(1)} %get-tuple-element.30), channel_id=1, source_target_pairs={{0,8},{8,0},{16,24},{24,16},{32,40},{40,32},{48,56},{56,48},{64,72... | collective-permute-start | bytes 589832 | tf_op jit(solution)/shard_map/ppermute | solution.py:402

commit v7 on v6

--- a/solution.py
+++ b/solution.py
@@ -266,33 +266,46 @@
     )(in_hbm(tokens), x, gathered, near, far)
 
 
-def middle_kernel(in_ref, back_ref, target_ref, student_ref, left_ref, out_ref):
+def left_terms(grads, turned, left_ref):
     par = parity()
     total = jnp.zeros((512, 128), F32)
-    turned = halves([in_ref[j] for j in range(8)])
-    outs = []
     for h in range(2):
-        lanes = slice(h * 512, (h + 1) * 512)
-        v = dot(turned[h], back_ref[h], ((1,), (1,)))
-        square = v * v
-        p = 0.5 + 0.5 * jnp.tanh(v * (ROOT + (ROOT * CUBE) * square))
-        act = v * p
-        slope = p + (act - act * p) * (2.0 * ROOT + (6.0 * ROOT * CUBE) * square)
-        student_ref[:, lanes] = act.astype(BF)
-        grad = ((act - target_ref[:, lanes].astype(F32)) * slope).astype(BF)
-        outs.append(dot(grad, back_ref[h]).astype(BF))
-        full = dot(grad, turned[h], ((0,), (0,)))
+        full = dot(grads[h], turned[h], ((0,), (0,)))
         full = jnp.where(same_block((512, 512)), full, 0.0).astype(BF)
         total = total + dot(full, spread(h, par), ((1,), (1,)))
-    low = iota((outs[0].shape[0], 128), 1) < 64
-    for p in range(4):
-        lanes = slice(p * 128, (p + 1) * 128)
-        a, b = outs[0][:, lanes], outs[1][:, lanes]
-        out_ref[2 * p] = jnp.where(low, a, b)
-        out_ref[2 * p + 1] = jnp.where(low, b, a)
     ordered = exchange(total, 8, 16)
     for s in range(16):
         left_ref[s] = ordered[s * 32 : (s + 1) * 32, :]
+
+
+def middle_kernel(in_ref, back_ref, target_ref, student_ref, left_ref, out_ref, grad_ref):
+    def work(later):
+        turned = halves([in_ref[j] for j in range(8)])
+        outs, grads = [], []
+        for h in range(2):
+            lanes = slice(h * 512, (h + 1) * 512)
+            v = dot(turned[h], back_ref[h], ((1,), (1,)))
+            square = v * v
+            p = 0.5 + 0.5 * jnp.tanh(v * (ROOT + (ROOT * CUBE) * square))
+            act = v * p
+            slope = p + (act - act * p) * (2.0 * ROOT + (6.0 * ROOT * CUBE) * square)
+            student_ref[:, lanes] = act.astype(BF)
+            grad = ((act - target_ref[:, lanes].astype(F32)) * slope).astype(BF)
+            outs.append(dot(grad, back_ref[h]).astype(BF))
+            grads.append(grad)
+            if not later:
+                grad_ref[:, lanes] = grad
+        low = iota((outs[0].shape[0], 128), 1) < 64
+        for p in range(4):
+            lanes = slice(p * 128, (p + 1) * 128)
+            a, b = outs[0][:, lanes], outs[1][:, lanes]
+            out_ref[2 * p] = jnp.where(low, a, b)
+            out_ref[2 * p + 1] = jnp.where(low, b, a)
+        if later:
+            left_terms(grads, turned, left_ref)
+
+    pl.when(core() == 0)(lambda: work(False))
+    pl.when(core() == 1)(lambda: work(True))
 
 
 def middle(received, back, target):
@@ -303,6 +316,7 @@
             pltpu.VMEM((rows, 1024), BF),
             jax.ShapeDtypeStruct((16, 32, 128), F32),
             jax.ShapeDtypeStruct((8, rows, 128), BF),
+            pltpu.VMEM((rows, 1024), BF),
         ),
         compiler_params=params(),
         cost_estimate=cost(2 * rows * 1024 * 1024, 10 * rows * 1024),
@@ -310,7 +324,10 @@
     )(received, back, target)
 
 
-def grads_kernel(student_ref, left_ref, back_ref, x_ref, student_hbm, mine_ref, other_ref, sem):
+def grads_kernel(
+    student_ref, left_in, grad_ref, in_ref, back_ref, x_ref,
+    student_hbm, mine_ref, other_ref, left_ref, sem,
+):
     copy = pltpu.make_async_copy(student_ref, student_hbm, sem)
     copy.start()
     same = flip() == 0
@@ -328,13 +345,22 @@
                 place = (chip(p, g, kh), slice(kh * 32, kh * 32 + 32))
                 mine_ref[place] = jnp.where(same, a, b)
                 other_ref[place] = jnp.where(same, b, a).astype(BF)
+    @pl.when(core() == 0)
+    def _():
+        turned = halves([in_ref[j] for j in range(8)])
+        left_terms([grad_ref[:, :512], grad_ref[:, 512:]], turned, left_ref)
+
+    @pl.when(core() == 1)
+    def _():
+        left_ref[...] = left_in[...]
+
     for n in range(8):
         mine_ref[n, 64:96, :] = left_ref[2 * n + core()]
         other_ref[n, 64:96, :] = left_ref[2 * n + 1 - core()].astype(BF)
     copy.wait()
 
 
-def grads(student, left, returned, x):
+def grads(student, left, grad, received, returned, x):
     rows = x.shape[0]
     return pl.pallas_call(
         grads_kernel,
@@ -344,11 +370,11 @@
             jax.ShapeDtypeStruct((8, 96, 128), BF),
         ),
         out_specs=(pl.BlockSpec(memory_space=pltpu.HBM), pl.BlockSpec(), pl.BlockSpec()),
-        scratch_shapes=[pltpu.SemaphoreType.DMA],
+        scratch_shapes=[pltpu.VMEM((16, 32, 128), F32), pltpu.SemaphoreType.DMA],
         compiler_params=params(),
         cost_estimate=cost(2 * rows * 1024 * 1024, 8 * rows * 1024),
         name="grads",
-    )(student, left, returned, x)
+    )(student, left, grad, received, returned, x)
 
 
 def sum_kernel(scale, in_ref, right_ref, left_ref):
@@ -396,9 +422,9 @@
     near = lax.cond(first, lambda share: share, gather_z, pass_on(share[:4], far))
     mixed, back = mix(tokens, x, gathered, near, far)
     received = lax.all_to_all(mixed, "blk", 0, 0, tiled=True)
-    student, left, out = middle(received, back, target)
+    student, left, out, grad = middle(received, back, target)
     returned = lax.all_to_all(out, "blk", 0, 0, tiled=True)
-    student, mine, other = grads(student, left, returned, tokens)
+    student, mine, other = grads(student, left, grad, received, returned, tokens)
     terms = (mine + lax.ppermute(other, "seq", across).astype(F32)).astype(BF)
     terms = lax.all_to_all(terms, "seq", 0, 0, tiled=True, axis_index_groups=chips)
     right_grad, left_grad = sums(terms, scale)

time: 101 us -> 99.5 us (0.985)
  blocking collectives: 77.9 us -> 76.4 us
    pallas_call x1, Pallas kernels: 1.36 us -> 3.27 us  [grads(): pl.pallas_call(grads_kernel, out_shape=(pltpu.HBM(student.shape, BF), jax...]
    all_to_all x1, blocking collectives: 24.2 us -> 22.8 us  [shards(): returned = lax.all_to_all(out, 'blk', 0, 0, tiled=True)]
    pallas_call x1, Pallas kernels: 5.4 us -> 4.13 us  [middle(): pl.pallas_call(middle_kernel, out_shape=(pltpu.VMEM((rows, 1024), BF), ja...]
where the time goes in v7:
time: 99.5 us; the launch traced here: 99.1 us
  blocking collectives  76.4 us (77%)
  Pallas kernels  12.2 us (12%)
  starting transfers between devices  7.51 us (8%)
  waiting for transfers between devices  2.09 us (2%)
    all_to_all x1, blocking collectives, shards(): received = lax.all_to_all(mixed, 'blk', 0, 0, tiled=True)  24.6 us
    all_to_all x1, blocking collectives, shards(): returned = lax.all_to_all(out, 'blk', 0, 0, tiled=True)  22.8 us
    all_to_all x1, blocking collectives, gather(): lax.all_to_all(share, 'seq', 0, 0, tiled=True, axis_index_groups=chips)  17.4 us
    all_to_all x1, blocking collectives, shards(): lax.all_to_all(terms, 'seq', 0, 0, tiled=True, axis_index_groups=chips)  11.7 us
    ppermute x1, starting transfers between devices, shards(): terms = (mine + lax.ppermute(other, 'seq', across).astype(F32)).astype(BF)  6.12 us
    pallas_call x1, Pallas kernels, middle(): pl.pallas_call(middle_kernel, out_shape=(pltpu.VMEM((rows, 1024), BF), ja...  4.13 us
    pallas_call x1, Pallas kernels, grads(): pl.pallas_call(grads_kernel, out_shape=(pltpu.HBM(student.shape, BF), jax...  3.27 us
  transfers between devices with their start and end apart: 3, of which 2 were waited for; matrix products, arithmetic and copies ran while one was open for 0% of the time, Pallas kernels for 2%

profile of v7, /device:TPU:0, one launch (start us, length us, event | category | flops | bytes accessed | tf_op | source)
XLA Modules:
  0.0 99.1 jit_solution(150880434654231753)
XLA Ops:
  0.6 0.8 pack.1.after_ref.own_ref
  1.5 0.1 collective-permute-start
  1.6 1.6 %fetch.1.after_ref.x_ref = bf16[1024,1024]{1,0:T(8,128)(2,1)S(1)} custom-call(bf16[1024,1024]{1,0:T(8,128)(2,1)} %x_ref.1, bf16[96,128]{1,0:T(8,128)(2,1)S(1)} %pack.1.after_ref.own_ref), custom_call_target="tpu_custom_call" | custom-call | bytes 8388608 | tf_op jit(solution)/shard_map/fetch/pallas_call | solution.py:191
  3.2 0.0 collective-permute-done.sib_ref
  3.3 17.5 %conditional.2 = (bf16[8,192,128]{2,1,0:T(8,128)(2,1)S(1)}) conditional(s32[]{:T(128)} %convert_element_type.10, bf16[8,192,128]{2,1,0:T(8,128)(2,1)S(1)} %pair.1, bf16[8,192,128]{2,1,0:T(8,128)(2,1)S(1)} %pair.1), branch_computations={%region_0.1_spmd, %region_1.2_spmd} | conditional | bytes 786440 | solution.py:420
  3.3 17.4 %all_to_all.23 = bf16[8,192,128]{2,1,0:T(8,128)(2,1)S(1)} all-to-all(bf16[8,192,128]{2,1,0:T(8,128)(2,1)S(1)} %param.1), channel_id=1, replica_groups={{0,16,32,48,64,80,96,112},{8,24,40,56,72,88,104,120},{1,17,33,49,65,81,..., dimensions={0} | all-to-all | bytes 786432 | tf_op jit(solution)/shard_map/cond/branch_1_fun/all_to_all | solution.py:413
  20.7 1.3 %collective-permute-start.1 = (bf16[4,192,128]{2,1,0:T(8,128)(2,1)S(1)}, bf16[4,192,128]{2,1,0:T(8,128)(2,1)S(1)}, u32[]{:S(2)}, u32[]{:S(2)}) collective-permute-start(bf16[4,192,128]{2,1,0:T(8,128)(2,1)S(1)} %other_half.1), channel_id=1, source_target_pairs={{0,8},{16,24},{32,40},{48,56},{64,72},{80,88},{96,104},{112,120},{... | collective-permute-start | bytes 589832 | tf_op jit(solution)/shard_map/ppermute | solution.py:421
  22.1 1.0 %collective-permute-done.1.turn_ref.far_ref = bf16[4,192,128]{2,1,0:T(8,128)(2,1)S(1)} collective-permute-done((bf16[4,192,128]{2,1,0:T(8,128)(2,1)S(1)}, bf16[4,192,128]{2,1,0:T(8,128)(2,1)S(1)}, u32[]{:S(2)}, u32[]{:S(2)}) %collective-permute-start.1) | collective-permute-done | bytes 196640 | tf_op jit(solution)/shard_map/ppermute | solution.py:421
  23.1 1.6 %mix.1 = (bf16[8,1024,128]{2,1,0:T(8,128)(2,1)S(1)}, bf16[2,512,512]{2,1,0:T(8,128)(2,1)S(1)}) custom-call(bf16[1024,1024]{1,0:T(8,128)(2,1)} %x_ref.1, bf16[1024,1024]{1,0:T(8,128)(2,1)S(1)} %fetch.1.after_ref.x_ref, bf16[8,192,128]{2,1,0:T(8,128)(2,1)S(1)} %get-tuple-element.35.g_ref.all_ref, bf16[4,192,128]{2,1,0:T(8,128)(2,1)S(1)} %get-tuple-element.36.near_ref, ...), custom_call_target="tpu_custom_call" | custom-call | flops 1073741824 | bytes 4194304 | tf_op jit(solution)/shard_map/mix/pallas_call | solution.py:251
  24.7 0.0 copy-start.1
  24.7 24.6 %all_to_all.25.in_ref = bf16[8,1024,128]{2,1,0:T(8,128)(2,1)S(1)} all-to-all(bf16[8,1024,128]{2,1,0:T(8,128)(2,1)S(1)} %get-tuple-element.24), channel_id=1, replica_groups=mesh['seq'=16,'blk'=8] {'blk'}, dimensions={0} | all-to-all | bytes 4194304 | tf_op jit(solution)/shard_map/all_to_all | solution.py:424
  49.3 0.0 copy-done.1
  49.3 4.1 %middle.1 = (bf16[1024,1024]{1,0:T(8,128)(2,1)S(1)}, f32[16,32,128]{2,1,0:T(8,128)S(1)}, bf16[8,1024,128]{2,1,0:T(8,128)(2,1)S(1)}, bf16[1024,1024]{1,0:T(8,128)(2,1)S(1)}) custom-call(bf16[8,1024,128]{2,1,0:T(8,128)(2,1)S(1)} %all_to_all.25.in_ref, bf16[2,512,512]{2,1,0:T(8,128)(2,1)S(1)} %get-tuple-element.25.back_ref, bf16[1024,1024]{1,0:T(8,128)(2,1)S(1)} %copy-done.1), custom_call_target="tpu_custom_call" | custom-call | flops 2147483648 | bytes 10485760 | tf_op jit(solution)/shard_map/middle/pallas_call | solution.py:313
  53.4 0.0 copy-start
  53.4 22.8 %all_to_all.26.back_ref = bf16[8,1024,128]{2,1,0:T(8,128)(2,1)S(1)} all-to-all(bf16[8,1024,128]{2,1,0:T(8,128)(2,1)S(1)} %get-tuple-element.29), channel_id=1, replica_groups=mesh['seq'=16,'blk'=8] {'blk'}, dimensions={0} | all-to-all | bytes 4194304 | tf_op jit(solution)/shard_map/all_to_all | solution.py:426
  76.2 0.0 copy-done
  76.2 3.3 %grads.1 = (bf16[1024,1024]{1,0:T(8,128)(2,1)}, f32[8,96,128]{2,1,0:T(8,128)S(1)}, bf16[8,96,128]{2,1,0:T(8,128)(2,1)S(1)}) custom-call(bf16[1024,1024]{1,0:T(8,128)(2,1)S(1)} %get-tuple-element.26.student_ref, f32[16,32,128]{2,1,0:T(8,128)S(1)} %get-tuple-element.27.left_in, bf16[1024,1024]{1,0:T(8,128)(2,1)S(1)} %get-tuple-element.28.grad_ref, ...), custom_call_target="tpu_custom_call" | custom-call | flops 2147483648 | bytes 8388608 | tf_op jit(solution)/shard_map/grads/pallas_call | solution.py:365
  79.5 6.1 %collective-permute-start.2 = (bf16[8,96,128]{2,1,0:T(8,128)(2,1)S(1)}, bf16[8,96,128]{2,1,0:T(8,128)(2,1)S(1)}, u32[]{:S(2)}, u32[]{:S(2)}) collective-permute-start(bf16[8,96,128]{2,1,0:T(8,128)(2,1)S(1)} %get-tuple-element.32), channel_id=1, source_target_pairs={{0,8},{8,0},{16,24},{24,16},{32,40},{40,32},{48,56},{56,48},{64,72... | collective-permute-start | bytes 589832 | tf_op jit(solution)/shard_map/ppermute | solution.py:428
  85.6 1.1 %collective-permute-done.2 = bf16[8,96,128]{2,1,0:T(8,128)(2,1)S(1)} collective-permute-done((bf16[8,96,128]{2,1,0:T(8,128)(2,1)S(1)}, bf16[8,96,128]{2,1,0:T(8,128)(2,1)S(1)}, u32[]{:S(2)}, u32[]{:S(2)}) %collective-permute-start.2) | collective-permute-done | bytes 196640 | tf_op jit(solution)/shard_map/ppermute | solution.py:428
  86.7 11.7 %all_to_all.27.in_ref = bf16[8,96,128]{2,1,0:T(8,128)(2,1)S(1)} all-to-all(bf16[8,96,128]{2,1,0:T(8,128)(2,1)S(1)} %add_convert_fusion), channel_id=1, replica_groups={{0,16,32,48,64,80,96,112},{8,24,40,56,72,88,104,120},{1,17,33,49,65,81,..., dimensions={0} | all-to-all | bytes 393216 | tf_op jit(solution)/shard_map/all_to_all | solution.py:429
  98.4 0.7 sums.1
  (6 shorter events, 0.1 us)
Async XLA Ops:
  1.5 1.7 %collective-permute-start = (bf16[96,128]{1,0:T(8,128)(2,1)S(1)}, bf16[96,128]{1,0:T(8,128)(2,1)S(1)}, u32[]{:S(2)}, u32[]{:S(2)}) collective-permute-start(bf16[96,128]{1,0:T(8,128)(2,1)S(1)} %pack.1.after_ref.own_ref), channel_id=1, source_target_pairs={{0,8},{8,0},{16,24},{24,16},{32,40},{40,32},{48,56},{56,48},{64,72... | collective-permute-start | bytes 73736 | tf_op jit(solution)/shard_map/ppermute | solution.py:410
  20.7 2.4 %collective-permute-start.1 = (bf16[4,192,128]{2,1,0:T(8,128)(2,1)S(1)}, bf16[4,192,128]{2,1,0:T(8,128)(2,1)S(1)}, u32[]{:S(2)}, u32[]{:S(2)}) collective-permute-start(bf16[4,192,128]{2,1,0:T(8,128)(2,1)S(1)} %other_half.1), channel_id=1, source_target_pairs={{0,8},{16,24},{32,40},{48,56},{64,72},{80,88},{96,104},{112,120},{... | collective-permute-start | bytes 589832 | tf_op jit(solution)/shard_map/ppermute | solution.py:421
  24.7 24.6 %copy-start.1 = (bf16[1024,1024]{1,0:T(8,128)(2,1)S(1)}, bf16[1024,1024]{1,0:T(8,128)(2,1)}, u32[]{:S(2)}) copy-start(bf16[1024,1024]{1,0:T(8,128)(2,1)} %target_ref.1) | copy-start | bytes 6291460
  53.4 22.8 %copy-start = (bf16[1024,1024]{1,0:T(8,128)(2,1)S(1)}, bf16[1024,1024]{1,0:T(8,128)(2,1)}, u32[]{:S(2)}) copy-start(bf16[1024,1024]{1,0:T(8,128)(2,1)} %x_ref.1) | copy-start | bytes 6291460
  79.5 7.2 %collective-permute-start.2 = (bf16[8,96,128]{2,1,0:T(8,128)(2,1)S(1)}, bf16[8,96,128]{2,1,0:T(8,128)(2,1)S(1)}, u32[]{:S(2)}, u32[]{:S(2)}) collective-permute-start(bf16[8,96,128]{2,1,0:T(8,128)(2,1)S(1)} %get-tuple-element.32), channel_id=1, source_target_pairs={{0,8},{8,0},{16,24},{24,16},{32,40},{40,32},{48,56},{56,48},{64,72... | collective-permute-start | bytes 589832 | tf_op jit(solution)/shard_map/ppermute | solution.py:428

commit v8 on v7

--- a/solution.py
+++ b/solution.py
@@ -199,7 +199,7 @@
     )(in_hbm(x), after)
 
 
-def mix_body(x_ref, g_ref, out_ref, back_ref):
+def back_body(g_ref, back_ref):
     par = parity()
     packed = jnp.concatenate(
         [g_ref[n, c * 96 + 64 : c * 96 + 96, :].astype(F32) for n in range(8) for c in range(2)],
@@ -209,6 +209,10 @@
     for h in range(2):
         full = dot(ordered, spread(h, par))
         back_ref[h] = jnp.where(same_block((512, 512)), full, 0.0).astype(BF)
+
+
+def mix_body(x_ref, g_ref, out_ref):
+    par = parity()
     lane_k = (iota((128, 512), 1) >> 3) & 3
     mixed = []
     for kh in range(2):
@@ -232,7 +236,8 @@
 def mix_kernel(x_hbm, x_ref, all_ref, near_ref, far_ref, out_ref, back_ref, g_ref, late_ref, sem):
     @pl.when(core() == 0)
     def _():
-        mix_body(x_ref, all_ref, out_ref, back_ref)
+        mix_body(x_ref, all_ref, out_ref)
+        back_body(all_ref, back_ref)
 
     @pl.when(core() == 1)
     def _():
@@ -242,8 +247,9 @@
         for z in range(4):
             g_ref[2 * z + here] = near_ref[z]
             g_ref[2 * z + 1 - here] = far_ref[z]
+        back_body(g_ref, back_ref)
         copy.wait()
-        mix_body(late_ref, g_ref, out_ref, back_ref)
+        mix_body(late_ref, g_ref, out_ref)
 
 
 def mix(tokens, x, gathered, near, far):

time: 99.5 us -> 100 us (level)
  blocking collectives: 76.4 us -> 77.9 us
where the time goes in v8:
time: 100 us; the launch traced here: 99.7 us
  blocking collectives  77.9 us (78%)
  Pallas kernels  12.3 us (12%)
  starting transfers between devices  6.52 us (7%)
  waiting for transfers between devices  2.09 us (2%)
    all_to_all x1, blocking collectives, shards(): received = lax.all_to_all(mixed, 'blk', 0, 0, tiled=True)  25.1 us
    all_to_all x1, blocking collectives, shards(): returned = lax.all_to_all(out, 'blk', 0, 0, tiled=True)  23.8 us
    all_to_all x1, blocking collectives, gather(): lax.all_to_all(share, 'seq', 0, 0, tiled=True, axis_index_groups=chips)  17.4 us
    all_to_all x1, blocking collectives, shards(): lax.all_to_all(terms, 'seq', 0, 0, tiled=True, axis_index_groups=chips)  11.7 us
    ppermute x1, starting transfers between devices, shards(): terms = (mine + lax.ppermute(other, 'seq', across).astype(F32)).astype(BF)  5.13 us
    pallas_call x1, Pallas kernels, middle(): pl.pallas_call(middle_kernel, out_shape=(pltpu.VMEM((rows, 1024), BF), ja...  4.13 us
    pallas_call x1, Pallas kernels, grads(): pl.pallas_call(grads_kernel, out_shape=(pltpu.HBM(student.shape, BF), jax...  3.27 us
  transfers between devices with their start and end apart: 3, of which 2 were waited for; matrix products, arithmetic and copies ran while one was open for 0% of the time, Pallas kernels for 2%

profile of v8, /device:TPU:0, one launch (start us, length us, event | category | flops | bytes accessed | tf_op | source)
XLA Modules:
  0.0 99.7 jit_solution(11646887595204902991)
XLA Ops:
  0.6 0.8 pack.1.after_ref.own_ref
  1.5 0.1 collective-permute-start
  1.6 1.6 %fetch.1.after_ref.x_ref = bf16[1024,1024]{1,0:T(8,128)(2,1)S(1)} custom-call(bf16[1024,1024]{1,0:T(8,128)(2,1)} %x_ref.1, bf16[96,128]{1,0:T(8,128)(2,1)S(1)} %pack.1.after_ref.own_ref), custom_call_target="tpu_custom_call" | custom-call | bytes 8388608 | tf_op jit(solution)/shard_map/fetch/pallas_call | solution.py:191
  3.2 0.0 collective-permute-done.sib_ref
  3.3 17.5 %conditional.2 = (bf16[8,192,128]{2,1,0:T(8,128)(2,1)S(1)}) conditional(s32[]{:T(128)} %convert_element_type.10, bf16[8,192,128]{2,1,0:T(8,128)(2,1)S(1)} %pair.1, bf16[8,192,128]{2,1,0:T(8,128)(2,1)S(1)} %pair.1), branch_computations={%region_0.1_spmd, %region_1.2_spmd} | conditional | bytes 786440 | solution.py:426
  3.3 17.4 %all_to_all.23 = bf16[8,192,128]{2,1,0:T(8,128)(2,1)S(1)} all-to-all(bf16[8,192,128]{2,1,0:T(8,128)(2,1)S(1)} %param.1), channel_id=1, replica_groups={{0,16,32,48,64,80,96,112},{8,24,40,56,72,88,104,120},{1,17,33,49,65,81,..., dimensions={0} | all-to-all | bytes 786432 | tf_op jit(solution)/shard_map/cond/branch_1_fun/all_to_all | solution.py:419
  20.7 1.3 %collective-permute-start.1 = (bf16[4,192,128]{2,1,0:T(8,128)(2,1)S(1)}, bf16[4,192,128]{2,1,0:T(8,128)(2,1)S(1)}, u32[]{:S(2)}, u32[]{:S(2)}) collective-permute-start(bf16[4,192,128]{2,1,0:T(8,128)(2,1)S(1)} %other_half.1), channel_id=1, source_target_pairs={{0,8},{16,24},{32,40},{48,56},{64,72},{80,88},{96,104},{112,120},{... | collective-permute-start | bytes 589832 | tf_op jit(solution)/shard_map/ppermute | solution.py:427
  22.1 1.0 %collective-permute-done.1.turn_ref.far_ref = bf16[4,192,128]{2,1,0:T(8,128)(2,1)S(1)} collective-permute-done((bf16[4,192,128]{2,1,0:T(8,128)(2,1)S(1)}, bf16[4,192,128]{2,1,0:T(8,128)(2,1)S(1)}, u32[]{:S(2)}, u32[]{:S(2)}) %collective-permute-start.1) | collective-permute-done | bytes 196640 | tf_op jit(solution)/shard_map/ppermute | solution.py:427
  23.1 1.7 %mix.1 = (bf16[8,1024,128]{2,1,0:T(8,128)(2,1)S(1)}, bf16[2,512,512]{2,1,0:T(8,128)(2,1)S(1)}) custom-call(bf16[1024,1024]{1,0:T(8,128)(2,1)} %x_ref.1, bf16[1024,1024]{1,0:T(8,128)(2,1)S(1)} %fetch.1.after_ref.x_ref, bf16[8,192,128]{2,1,0:T(8,128)(2,1)S(1)} %get-tuple-element.35.g_ref.all_ref, bf16[4,192,128]{2,1,0:T(8,128)(2,1)S(1)} %get-tuple-element.36.near_ref, ...), custom_call_target="tpu_custom_call" | custom-call | flops 1073741824 | bytes 4194304 | tf_op jit(solution)/shard_map/mix/pallas_call | solution.py:257
  24.8 0.0 copy-start.1
  24.8 25.1 %all_to_all.25.in_ref = bf16[8,1024,128]{2,1,0:T(8,128)(2,1)S(1)} all-to-all(bf16[8,1024,128]{2,1,0:T(8,128)(2,1)S(1)} %get-tuple-element.24), channel_id=1, replica_groups=mesh['seq'=16,'blk'=8] {'blk'}, dimensions={0} | all-to-all | bytes 4194304 | tf_op jit(solution)/shard_map/all_to_all | solution.py:430
  49.9 0.0 copy-done.1
  49.9 4.1 %middle.1 = (bf16[1024,1024]{1,0:T(8,128)(2,1)S(1)}, f32[16,32,128]{2,1,0:T(8,128)S(1)}, bf16[8,1024,128]{2,1,0:T(8,128)(2,1)S(1)}, bf16[1024,1024]{1,0:T(8,128)(2,1)S(1)}) custom-call(bf16[8,1024,128]{2,1,0:T(8,128)(2,1)S(1)} %all_to_all.25.in_ref, bf16[2,512,512]{2,1,0:T(8,128)(2,1)S(1)} %get-tuple-element.25.back_ref, bf16[1024,1024]{1,0:T(8,128)(2,1)S(1)} %copy-done.1), custom_call_target="tpu_custom_call" | custom-call | flops 2147483648 | bytes 10485760 | tf_op jit(solution)/shard_map/middle/pallas_call | solution.py:319
  54.0 0.0 copy-start
  54.1 23.8 %all_to_all.26.back_ref = bf16[8,1024,128]{2,1,0:T(8,128)(2,1)S(1)} all-to-all(bf16[8,1024,128]{2,1,0:T(8,128)(2,1)S(1)} %get-tuple-element.29), channel_id=1, replica_groups=mesh['seq'=16,'blk'=8] {'blk'}, dimensions={0} | all-to-all | bytes 4194304 | tf_op jit(solution)/shard_map/all_to_all | solution.py:432
  77.8 0.0 copy-done
  77.8 3.3 %grads.1 = (bf16[1024,1024]{1,0:T(8,128)(2,1)}, f32[8,96,128]{2,1,0:T(8,128)S(1)}, bf16[8,96,128]{2,1,0:T(8,128)(2,1)S(1)}) custom-call(bf16[1024,1024]{1,0:T(8,128)(2,1)S(1)} %get-tuple-element.26.student_ref, f32[16,32,128]{2,1,0:T(8,128)S(1)} %get-tuple-element.27.left_in, bf16[1024,1024]{1,0:T(8,128)(2,1)S(1)} %get-tuple-element.28.grad_ref, ...), custom_call_target="tpu_custom_call" | custom-call | flops 2147483648 | bytes 8388608 | tf_op jit(solution)/shard_map/grads/pallas_call | solution.py:371
  81.1 5.1 %collective-permute-start.2 = (bf16[8,96,128]{2,1,0:T(8,128)(2,1)S(1)}, bf16[8,96,128]{2,1,0:T(8,128)(2,1)S(1)}, u32[]{:S(2)}, u32[]{:S(2)}) collective-permute-start(bf16[8,96,128]{2,1,0:T(8,128)(2,1)S(1)} %get-tuple-element.32), channel_id=1, source_target_pairs={{0,8},{8,0},{16,24},{24,16},{32,40},{40,32},{48,56},{56,48},{64,72... | collective-permute-start | bytes 589832 | tf_op jit(solution)/shard_map/ppermute | solution.py:434
  86.2 1.1 %collective-permute-done.2 = bf16[8,96,128]{2,1,0:T(8,128)(2,1)S(1)} collective-permute-done((bf16[8,96,128]{2,1,0:T(8,128)(2,1)S(1)}, bf16[8,96,128]{2,1,0:T(8,128)(2,1)S(1)}, u32[]{:S(2)}, u32[]{:S(2)}) %collective-permute-start.2) | collective-permute-done | bytes 196640 | tf_op jit(solution)/shard_map/ppermute | solution.py:434
  87.4 11.7 %all_to_all.27.in_ref = bf16[8,96,128]{2,1,0:T(8,128)(2,1)S(1)} all-to-all(bf16[8,96,128]{2,1,0:T(8,128)(2,1)S(1)} %add_convert_fusion), channel_id=1, replica_groups={{0,16,32,48,64,80,96,112},{8,24,40,56,72,88,104,120},{1,17,33,49,65,81,..., dimensions={0} | all-to-all | bytes 393216 | tf_op jit(solution)/shard_map/all_to_all | solution.py:435
  99.0 0.7 sums.1
  (6 shorter events, 0.1 us)
Async XLA Ops:
  1.5 1.7 %collective-permute-start = (bf16[96,128]{1,0:T(8,128)(2,1)S(1)}, bf16[96,128]{1,0:T(8,128)(2,1)S(1)}, u32[]{:S(2)}, u32[]{:S(2)}) collective-permute-start(bf16[96,128]{1,0:T(8,128)(2,1)S(1)} %pack.1.after_ref.own_ref), channel_id=1, source_target_pairs={{0,8},{8,0},{16,24},{24,16},{32,40},{40,32},{48,56},{56,48},{64,72... | collective-permute-start | bytes 73736 | tf_op jit(solution)/shard_map/ppermute | solution.py:416
  20.7 2.4 %collective-permute-start.1 = (bf16[4,192,128]{2,1,0:T(8,128)(2,1)S(1)}, bf16[4,192,128]{2,1,0:T(8,128)(2,1)S(1)}, u32[]{:S(2)}, u32[]{:S(2)}) collective-permute-start(bf16[4,192,128]{2,1,0:T(8,128)(2,1)S(1)} %other_half.1), channel_id=1, source_target_pairs={{0,8},{16,24},{32,40},{48,56},{64,72},{80,88},{96,104},{112,120},{... | collective-permute-start | bytes 589832 | tf_op jit(solution)/shard_map/ppermute | solution.py:427
  24.8 25.1 %copy-start.1 = (bf16[1024,1024]{1,0:T(8,128)(2,1)S(1)}, bf16[1024,1024]{1,0:T(8,128)(2,1)}, u32[]{:S(2)}) copy-start(bf16[1024,1024]{1,0:T(8,128)(2,1)} %target_ref.1) | copy-start | bytes 6291460
  54.0 23.8 %copy-start = (bf16[1024,1024]{1,0:T(8,128)(2,1)S(1)}, bf16[1024,1024]{1,0:T(8,128)(2,1)}, u32[]{:S(2)}) copy-start(bf16[1024,1024]{1,0:T(8,128)(2,1)} %x_ref.1) | copy-start | bytes 6291460
  81.1 6.2 %collective-permute-start.2 = (bf16[8,96,128]{2,1,0:T(8,128)(2,1)S(1)}, bf16[8,96,128]{2,1,0:T(8,128)(2,1)S(1)}, u32[]{:S(2)}, u32[]{:S(2)}) collective-permute-start(bf16[8,96,128]{2,1,0:T(8,128)(2,1)S(1)} %get-tuple-element.32), channel_id=1, source_target_pairs={{0,8},{8,0},{16,24},{24,16},{32,40},{40,32},{48,56},{56,48},{64,72... | collective-permute-start | bytes 589832 | tf_op jit(solution)/shard_map/ppermute | solution.py:434
